TPU v7x, 256 devices: a whole 4x4x8 slice. The times are simulated.
256 devices in a mesh: grp: 32 (over z, y), mem: 8 (over x, core).
Axes of the slice: x: 4, y: 4, z: 8, core: 2. Of those that a mesh axis runs over, the one named last changes fastest.
Arguments:
- tokens: bfloat16 [4096, 3584], P(('grp', 'mem')), may hold values from -6 to 6
- expert_ids: int32 [4096, 8], P(('grp', 'mem')), may hold values from 0 to 127, as said below
- gates: float32 [4096, 8], P(('grp', 'mem')), may hold values from 0.1 to 0.6
- gate_weight: bfloat16 [256, 3584, 512], P(('grp', 'mem')), may hold values from -0.09375 to 0.09375
- up_weight: bfloat16 [256, 3584, 512], P(('grp', 'mem')), may hold values from -0.09375 to 0.09375
- down_weight: bfloat16 [256, 512, 3584], P(('grp', 'mem')), may hold values from -0.1875 to 0.1875
Outputs:
- mixed: bfloat16 [4096, 3584], P(('grp', 'mem'))
Inputs may be any that keep to these rules, and one draw needn't show every extreme that they name: `expert_ids`: each row names 8 different experts, all within at most 4 of the 8 groups of 16 consecutive experts. The rows of one device (aligned blocks of 16 rows) name no expert more than 2 times, and there is at least one expert (the same one in every block) that every such block names exactly 2 times.
All inputs are finite; a program needn't handle non-finite values.
Results may differ from a plain program's by a relative error of at most 0.0065.
Values may be sent and summed in bfloat16 or wider, within the bound.
No kernel may reach another device: no remote copies, remote signals or barrier semaphores. Data moves between devices by JAX's collectives and lax.ppermute only.
A program may use at most 64 MiB of HBM per device.

v0:
```python
import jax
import jax.numpy as jnp
from jax import lax
from jax.sharding import PartitionSpec as P


def expert_half(block_rows, gate_half, up_half, down_half):
    block_shape = block_rows.shape
    flat_rows = block_rows.reshape(-1, block_shape[-1])
    gate_proj = jnp.dot(flat_rows, gate_half, preferred_element_type=jnp.float32)
    up_proj = jnp.dot(flat_rows, up_half, preferred_element_type=jnp.float32)
    hidden = (jax.nn.silu(gate_proj) * up_proj).astype(jnp.bfloat16)
    half_out = jnp.dot(hidden, down_half, preferred_element_type=jnp.float32).astype(jnp.bfloat16)
    return half_out.reshape(block_shape)


def body(tokens, expert_ids, gates, gate_weight, up_weight, down_weight):
    grp_count = lax.axis_size("grp")
    mem_count = lax.axis_size("mem")
    experts = grp_count * mem_count // 2
    per_grp = mem_count // 2
    row_count = tokens.shape[0]
    model_width = tokens.shape[1]
    top_count = expert_ids.shape[1]
    slot_count = 2 * row_count * top_count // experts
    gate_half = gate_weight[0]
    up_half = up_weight[0]
    down_half = down_weight[0]
    flat_ids = expert_ids.reshape(-1)
    onehot = (flat_ids[:, None] == jnp.arange(experts, dtype=jnp.int32)[None, :]).astype(jnp.int32)
    earlier = jnp.cumsum(onehot, axis=0) - onehot
    slot_index = jnp.sum(onehot * earlier, axis=1)
    position = flat_ids * slot_count + slot_index
    pair_source = jnp.arange(row_count * top_count, dtype=jnp.int32) // top_count + 1
    source_row = jnp.zeros((experts * slot_count,), jnp.int32).at[position].set(pair_source)
    rows_padded = jnp.concatenate([jnp.zeros((1, model_width), tokens.dtype), tokens], axis=0)
    outgoing = rows_padded[source_row].reshape(grp_count, per_grp * slot_count, model_width)
    arrived = lax.all_to_all(outgoing, "grp", split_axis=0, concat_axis=0, tiled=True)
    arrived = arrived.reshape(grp_count, per_grp, 1, slot_count, model_width)
    doubled = jnp.broadcast_to(arrived, (grp_count, per_grp, 2, slot_count, model_width))
    doubled = doubled.reshape(grp_count, mem_count, slot_count, model_width)
    partial_value = expert_half(
        lax.all_to_all(doubled, "mem", split_axis=1, concat_axis=1, tiled=True),
        gate_half,
        up_half,
        down_half,
    )
    returned_rows = lax.all_to_all(partial_value, "mem", split_axis=1, concat_axis=1, tiled=True)
    returned_rows = returned_rows.reshape(grp_count, per_grp, 2, slot_count, model_width)
    summed = (
        returned_rows[:, :, 0].astype(jnp.float32) + returned_rows[:, :, 1].astype(jnp.float32)
    ).astype(jnp.bfloat16)
    homeward = summed.reshape(grp_count, per_grp * slot_count, model_width)
    result_rows = lax.all_to_all(homeward, "grp", split_axis=0, concat_axis=0, tiled=True)
    result_table = result_rows.reshape(experts * slot_count, model_width)
    picked = result_table[position].astype(jnp.float32).reshape(row_count, top_count, model_width)
    mixed = jnp.sum(gates[:, :, None] * picked, axis=1)
    return mixed.astype(jnp.bfloat16)


def solution(mesh):
    return jax.shard_map(
        body,
        mesh=mesh,
        in_specs=(
            P(("grp", "mem"), None),
            P(("grp", "mem"), None),
            P(("grp", "mem"), None),
            P(("grp", "mem"), None, None),
            P(("grp", "mem"), None, None),
            P(("grp", "mem"), None, None),
        ),
        out_specs=P(("grp", "mem"), None),
        check_vma=False,
    )
```

profile of v0, /device:TPU:1, one launch (start us, length us, event | category | flops | bytes accessed | tf_op | source)
XLA Modules:
  0.0 266.9 jit_solution(11981846575574745152)
XLA Ops:
  0.0 0.8 copy.36
  0.8 0.7 broadcast_multiply_fusion
  1.5 0.1 eq.15
  1.5 0.1 fusion.15
  1.6 0.2 reduce_window_sum.11
  1.8 0.2 select_reduce_fusion
  2.0 0.1 copy.35
  2.1 0.1 mul.37
  2.2 1.0 scatter_custom_fusion
  3.2 0.9 concatenate.3
  4.1 1.7 gather_fusion
  5.8 55.2 %all_to_all.20 = bf16[32,8,3584]{2,1,0:T(8,128)(2,1)} all-to-all(bf16[32,8,3584]{2,1,0:T(8,128)(2,1)S(1)} %bitcast.34), channel_id=1, replica_groups=mesh['grp'=32,'mem'=8] {'grp'}, dimensions={0} | all-to-all | bytes 3670016 | tf_op jit(solution)/shard_map/all_to_all | solution.py:38
  61.0 3.9 %broadcast_in_dim.7 = bf16[32,4,2,3584]{3,2,1,0:T(2,128)(2,1)S(1)} reshape(bf16[32,8,3584]{2,1,0:T(8,128)(2,1)} %all_to_all.20) | data formatting | bytes 3670016 | tf_op jit(solution)/shard_map/broadcast_in_dim | solution.py:40
  64.9 2.5 copy.37
  67.4 5.7 %broadcast_in_dim.8 = bf16[32,4,2,2,3584]{4,3,0,2,1:T(2,128)(2,1)} broadcast(bf16[32,4,2,3584]{3,2,0,1:T(2,128)(2,1)} %copy.37), dimensions={0,1,3,4} | broadcast | bytes 5505024 | tf_op jit(solution)/shard_map/broadcast_in_dim | solution.py:40
  73.1 51.4 %all_to_all.21 = bf16[32,8,2,3584]{3,2,0,1:T(2,128)(2,1)S(1)} all-to-all(bf16[32,8,2,3584]{3,2,0,1:T(2,128)(2,1)} %bitcast.32), channel_id=1, replica_groups=mesh['grp'=32,'mem'=8] {'mem'}, dimensions={1} | all-to-all | bytes 7340032 | tf_op jit(solution)/shard_map/all_to_all | solution.py:43
  124.5 5.7 %copy.38 = bf16[32,8,2,3584]{3,2,1,0:T(2,128)(2,1)} copy(bf16[32,8,2,3584]{3,2,0,1:T(2,128)(2,1)S(1)} %all_to_all.21) | data formatting | bytes 7340032 | tf_op jit(solution)/shard_map/all_to_all | solution.py:43
  130.2 8.4 %reshape.64 = bf16[512,3584]{1,0:T(8,128)(2,1)} reshape(bf16[32,8,2,3584]{3,2,1,0:T(2,128)(2,1)} %copy.38) | data formatting | bytes 7340032 | tf_op jit(solution)/shard_map/reshape | solution.py:9
  138.6 5.2 %fusion.3 = f32[512,512]{1,0:T(8,128)S(1)} fusion(bf16[512,3584]{1,0:T(8,128)(2,1)} %reshape.64, bf16[1,3584,512]{2,1,0:T(8,128)(2,1)} %param.9), kind=kOutput, calls=%fused_computation.7 | convolution fusion | flops 1879048192 | bytes 8388608 | tf_op jit(solution)/shard_map/dot_general | solution.py:10
  143.8 10.1 %convolution_convert_fusion = bf16[512,3584]{1,0:T(8,128)(2,1)} fusion(bf16[1,512,3584]{2,1,0:T(8,128)(2,1)} %param.11, bf16[512,3584]{1,0:T(8,128)(2,1)} %reshape.64, bf16[1,3584,512]{2,1,0:T(8,128)(2,1)} %param.10, f32[512,512]{1,0:T(8,128)S(1)} %fusion.3), kind=kOutput, calls=%fused_computation.3 | convolution fusion | flops 3761504256 | bytes 15728640 | tf_op jit(solution)/shard_map/dot_general | solution.py:13
  153.9 8.1 %reshape.65 = bf16[32,8,2,3584]{3,2,1,0:T(2,128)(2,1)} reshape(bf16[512,3584]{1,0:T(8,128)(2,1)} %convolution_convert_fusion) | data formatting | bytes 7340032 | tf_op jit(solution)/shard_map/reshape | solution.py:14
  162.0 4.6 %copy.39 = bf16[32,8,2,3584]{3,2,0,1:T(2,128)(2,1)S(1)} copy(bf16[32,8,2,3584]{3,2,1,0:T(2,128)(2,1)} %reshape.65) | data formatting | bytes 7340032 | tf_op jit(solution)/shard_map/reshape | solution.py:14
  166.6 47.1 %all_to_all.22 = bf16[32,8,2,3584]{3,2,0,1:T(2,128)(2,1)S(1)} all-to-all(bf16[32,8,2,3584]{3,2,0,1:T(2,128)(2,1)S(1)} %copy.39), channel_id=1, replica_groups=mesh['grp'=32,'mem'=8] {'mem'}, dimensions={1} | all-to-all | bytes 7340032 | tf_op jit(solution)/shard_map/all_to_all | solution.py:48
  213.7 0.6 copy.40
  214.3 0.5 add_convert_fusion
  214.7 0.0 copy-start
  214.8 2.3 copy.41
  217.0 4.4 %all-to-all-start.3 = ((bf16[32,8,3584]{2,1,0:T(8,128)(2,1)}), bf16[32,8,3584]{2,1,0:T(8,128)(2,1)S(1)}, u32[]{:S(2)}, u32[]{:S(2)}) async-start(bf16[32,8,3584]{2,1,0:T(8,128)(2,1)} %copy.41), calls=%async_computation.3 | async-start | bytes 3670016 | tf_op jit(solution)/shard_map/all_to_all | solution.py:54
  221.4 0.0 copy-done
  221.4 0.1 copy.34
  221.5 42.9 %all-to-all-done.3 = bf16[32,8,3584]{2,1,0:T(8,128)(2,1)S(1)} async-done(((bf16[32,8,3584]{2,1,0:T(8,128)(2,1)}), bf16[32,8,3584]{2,1,0:T(8,128)(2,1)S(1)}, u32[]{:S(2)}, u32[]{:S(2)}) %all-to-all-start.3) | async-done | bytes 1835040 | tf_op jit(solution)/shard_map/all_to_all | solution.py:54
  264.4 1.1 gather_fusion.1
  265.5 1.3 fusion.5
  (5 shorter events, 0.0 us)
Async XLA Ops:
  214.7 6.7 %copy-start = (f32[16,8]{0,1:T(8,128)S(1)}, f32[16,8]{0,1:T(8,128)}, u32[]{:S(2)}) copy-start(f32[16,8]{0,1:T(8,128)} %param.8) | copy-start | bytes 1540
  217.0 47.4 %all-to-all-start.3 = ((bf16[32,8,3584]{2,1,0:T(8,128)(2,1)}), bf16[32,8,3584]{2,1,0:T(8,128)(2,1)S(1)}, u32[]{:S(2)}, u32[]{:S(2)}) async-start(bf16[32,8,3584]{2,1,0:T(8,128)(2,1)} %copy.41), calls=%async_computation.3 | async-start | bytes 3670016 | tf_op jit(solution)/shard_map/all_to_all | solution.py:54
where the time goes:
time: 269 us; the launch traced here: 267 us
  blocking collectives  154 us (57%)
  local copies, waits for them, and re-layouts  47.5 us (18%)
  waiting for transfers between devices  42.9 us (16%)
  matrix products  15.3 us (6%)
  starting transfers between devices  4.41 us (2%)
  other arithmetic  2.95 us (1%)
    all_to_all x1, blocking collectives, body(): lax.all_to_all(outgoing, 'grp', split_axis=0, concat_axis=0, tiled=True)  55.2 us
    all_to_all x1, blocking collectives, body(): lax.all_to_all(doubled, 'mem', split_axis=1, concat_axis=1, tiled=True)  51.4 us
    all_to_all x1, blocking collectives, body(): lax.all_to_all(partial_value, 'mem', split_axis=1, concat_axis=1, tiled=T...  47.1 us
    all_to_all x1, waiting for transfers between devices, body(): lax.all_to_all(homeward, 'grp', split_axis=0, concat_axis=0, tiled=True)  42.9 us
    reshape x2, local copies, waits for them, and re-layouts, expert_half(): return half_out.reshape(block_shape)  12.7 us
    broadcast_in_dim x3, local copies, waits for them, and re-layouts, body(): jnp.broadcast_to(arrived, (grp_count, per_grp, 2, slot_count, model_width))  12 us
    dot_general x1, matrix products, expert_half(): jnp.dot(hidden, down_half, preferred_element_type=jnp.float32)  10.1 us
    reshape x1, local copies, waits for them, and re-layouts, expert_half(): flat_rows = block_rows.reshape(-1, block_shape[-1])  8.4 us
  transfers between devices with their start and end apart: 1, of which 1 were waited for; matrix products, arithmetic and copies ran while one was open for 0% of the time, Pallas kernels for 0%

commit v1 on v0

v1 whole, which is shorter than its diff:
```python
import jax
import jax.numpy as jnp
from jax import lax
from jax.experimental import pallas as pl
from jax.experimental.pallas import tpu as pltpu
from jax.sharding import Mesh, PartitionSpec as P

Z, Y, X, C = 8, 4, 4, 2
PLANE = Y * X
SLOTS = 2
TAIL = 128
BF = jnp.bfloat16
F32 = jnp.float32
MIB = 1 << 20


def along(shift):
    pairs = []
    for z in range(Z):
        pairs.append((z * C, (z + shift) % Z * C))
        pairs.append((z * C + 1, (z - shift) % Z * C + 1))
    return pairs


def send(value, shift):
    return lax.ppermute(value, ("z", "c"), along(shift))


def swap(value):
    return lax.ppermute(value, "c", [(0, 1), (1, 0)])


def place_kernel(own, near, second, third, fourth, rows_out, high_out, low_out):
    pieces = (own, near, second, third, fourth)
    width = rows_out.shape[1]
    rows = sum(p.shape[0] for p in pieces)
    block = own.shape[0]
    blocks = rows // block
    per_expert = blocks * SLOTS
    slots = PLANE * per_expert
    tail = jnp.concatenate([p[:, width:] for p in pieces], axis=0).astype(F32).T
    expert = (lax.axis_index("z") * PLANE + lax.broadcasted_iota(jnp.int32, (PLANE, rows), 0)).astype(F32)
    named = jnp.zeros((PLANE, rows), F32)
    gate = jnp.zeros((PLANE, rows), F32)
    for k in range(8):
        hit = tail[k : k + 1] == expert
        value = tail[8 + k : 9 + k] + tail[16 + k : 17 + k] + tail[24 + k : 25 + k]
        named = named + jnp.where(hit, 1.0, 0.0)
        gate = gate + jnp.where(hit, value, 0.0)
    before = lax.broadcasted_iota(jnp.int32, (rows, rows), 0)
    after = lax.broadcasted_iota(jnp.int32, (rows, rows), 1)
    earlier = jnp.where((before < after) & (before // block == after // block), 1.0, 0.0).astype(BF)
    rank = jnp.dot(named.astype(BF), earlier, preferred_element_type=F32)

    def spread(value):
        return jnp.broadcast_to(value[:, None, :], (PLANE, per_expert, rows)).reshape(slots, rows)

    slot = lax.broadcasted_iota(jnp.int32, (slots, rows), 0)
    lane = lax.broadcasted_iota(jnp.int32, (slots, rows), 1)
    here = (slot // SLOTS) % blocks == lane // block
    chosen = here & (spread(named) > 0.5) & (spread(rank) == (slot % SLOTS).astype(F32))
    weight = jnp.where(chosen, spread(gate), 0.0)
    high = weight.astype(BF)
    high_out[...] = high
    low_out[...] = (weight - high.astype(F32)).astype(BF)
    pick = jnp.where(chosen, 1.0, 0.0).astype(BF)
    step = 512
    for c in range(0, width, step):
        part = jnp.concatenate([p[:, c : c + step] for p in pieces], axis=0)
        rows_out[:, c : c + step] = jnp.dot(pick, part, preferred_element_type=F32).astype(BF)


def place(pieces, width):
    rows = sum(p.shape[0] for p in pieces)
    slots = PLANE * SLOTS * (rows // pieces[0].shape[0])
    return pl.pallas_call(
        place_kernel,
        out_shape=(
            jax.ShapeDtypeStruct((slots, width), BF),
            jax.ShapeDtypeStruct((slots, rows), BF),
            jax.ShapeDtypeStruct((slots, rows), BF),
        ),
        compiler_params=pltpu.CompilerParams(vmem_limit_bytes=24 * MIB),
        name="place",
    )(*pieces)


def expert_kernel(rows, gate_a, up_a, down_a, gate_b, up_b, down_b, out, gate_v, up_v, down_v, hidden, sems):
    width, half = gate_a.shape
    tile = 256
    tiles = half // tile
    cut = width // 2
    ins = []
    for h, (g, u) in enumerate(((gate_a, up_a), (gate_b, up_b))):
        for j in range(tiles):
            where = pl.ds(j * tile, tile)
            for m, (src, dst) in enumerate(((g, gate_v), (u, up_v))):
                ins.append(pltpu.make_async_copy(src.at[:, where], dst.at[h, :, where], sems.at[(h * tiles + j) * 2 + m]))
    downs = []
    for j in range(2):
        for h, d in enumerate((down_a, down_b)):
            where = pl.ds(j * cut, cut)
            downs.append(pltpu.make_async_copy(d.at[:, where], down_v.at[pl.ds(h * half, half), where], sems.at[4 * tiles + j * 2 + h]))
    for copy in ins + downs:
        copy.start()
    for i in range(2 * tiles):
        h, j = i // tiles, i % tiles
        ins[2 * i].wait()
        ins[2 * i + 1].wait()
        g = jnp.dot(rows[...], gate_v[h, :, j * tile : (j + 1) * tile], preferred_element_type=F32)
        u = jnp.dot(rows[...], up_v[h, :, j * tile : (j + 1) * tile], preferred_element_type=F32)
        hidden[:, i * tile : (i + 1) * tile] = (g / (1.0 + jnp.exp(-g)) * u).astype(BF)
    step = 256
    for j in range(2):
        downs[2 * j].wait()
        downs[2 * j + 1].wait()
        for c in range(j * cut, (j + 1) * cut, step):
            out[:, c : c + step] = jnp.dot(hidden[...], down_v[:, c : c + step], preferred_element_type=F32).astype(BF)


def experts(rows, own, other):
    width, half = own[0].shape
    count = rows.shape[0]
    vmem = pl.BlockSpec(memory_space=pltpu.VMEM)
    anywhere = pl.BlockSpec(memory_space=pl.ANY)
    return pl.pallas_call(
        expert_kernel,
        out_shape=jax.ShapeDtypeStruct((count, width), BF),
        in_specs=[vmem] + [anywhere] * 6,
        out_specs=vmem,
        scratch_shapes=[
            pltpu.VMEM((2, width, half), BF),
            pltpu.VMEM((2, width, half), BF),
            pltpu.VMEM((2 * half, width), BF),
            pltpu.VMEM((count, 2 * half), BF),
            pltpu.SemaphoreType.DMA((4 * (half // 256) + 4,)),
        ],
        compiler_params=pltpu.CompilerParams(vmem_limit_bytes=40 * MIB),
        cost_estimate=pl.CostEstimate(
            flops=2 * count * width * half * 6, bytes_accessed=12 * width * half + 4 * count * width, transcendentals=2 * count * half
        ),
        name="experts",
    )(rows, *own, *other)


def collect_kernel(returned, high, low, own_out, near_out, second_out, third_out, fourth_out):
    width = returned.shape[1]
    step = 512
    across = (((0,), (0,)), ((), ()))
    for c in range(0, width, step):
        part = returned[:, c : c + step]
        total = lax.dot_general(high[...], part, across, preferred_element_type=F32)
        total = total + lax.dot_general(low[...], part, across, preferred_element_type=F32)
        start = 0
        for ref in (own_out, near_out, second_out, third_out, fourth_out):
            count = ref.shape[0]
            ref[:, c : c + step] = total[start : start + count].astype(ref.dtype)
            start += count


def collect(returned, high, low, block):
    width = returned.shape[1]

    def shape(blocks, kind):
        return jax.ShapeDtypeStruct((blocks * block, width), kind)

    return pl.pallas_call(
        collect_kernel,
        out_shape=(shape(1, F32), shape(2, BF), shape(2, F32), shape(2, BF), shape(1, BF)),
        compiler_params=pltpu.CompilerParams(vmem_limit_bytes=24 * MIB),
        name="collect",
    )(returned, high, low)


def body(tokens, expert_ids, gates, gate_weight, up_weight, down_weight):
    block, width = tokens.shape
    own_weights = (gate_weight[0], up_weight[0], down_weight[0])
    other_weights = tuple(swap(w) for w in own_weights)
    high = lax.reduce_precision(gates, 8, 7)
    rest = gates - high
    middle = lax.reduce_precision(rest, 8, 7)
    low = rest - middle
    used = 4 * expert_ids.shape[1]
    tail = [v.astype(BF) for v in (expert_ids, high, middle, low)] + [jnp.zeros((block, TAIL - used), BF)]
    own = jnp.concatenate([tokens] + tail, axis=1)
    both = jnp.concatenate([own, swap(own)], axis=0)
    second = send(both, 2)
    near = send(both, 1)
    third = send(second, 1)
    fourth = send(second[:block], 2)
    placed, weight_high, weight_low = place((own, near, second, third, fourth), width)
    arrived = lax.all_to_all(placed.reshape(PLANE, -1, width), ("y", "x"), 0, 0, tiled=True)
    done = experts(arrived.reshape(-1, width), own_weights, other_weights)
    returned = lax.all_to_all(done.reshape(PLANE, -1, width), ("y", "x"), 0, 0, tiled=True)
    q_own, q_near, q_second, q_third, q_fourth = collect(returned.reshape(-1, width), weight_high, weight_low, block)
    from_third = send(q_third, -1)
    from_fourth = send(q_fourth, -2)
    from_near = send(q_near, -1)
    first_half = q_second[:block] + from_third[:block].astype(F32) + from_fourth.astype(F32)
    second_half = q_second[block:] + from_third[block:].astype(F32)
    from_second = send(jnp.concatenate([first_half, second_half], axis=0).astype(BF), -2)
    total = from_near.astype(F32) + from_second.astype(F32)
    from_core = swap(total[block:].astype(BF))
    return (q_own + total[:block] + from_core.astype(F32)).astype(BF)


def solution(mesh):
    fine = Mesh(mesh.devices.reshape(Z, Y, X, C), ("z", "y", "x", "c"))
    rows = P(("z", "y", "x", "c"))
    return jax.shard_map(body, mesh=fine, in_specs=(rows,) * 6, out_specs=rows, check_vma=False)
```

time: 269 us -> 122 us (0.45)
  blocking collectives: 154 us -> 54.6 us
  local copies, waits for them, and re-layouts: 47.5 us -> 3.97 us
  starting transfers between devices: 4.41 us -> 24.7 us
  waiting for transfers between devices: 42.9 us -> 27.2 us
  matrix products: 15.3 us -> 0 us
  Pallas kernels: 0 us -> 9.15 us
    all_to_all x3 -> x2, blocking collectives: 154 us -> 54.6 us  [the longest x1 29.3 us: body(): lax.all_to_all(placed.reshape(PLANE, -1, width), ('y', 'x'), 0, 0, tiled=...]
    all_to_all x1 -> x0, waiting for transfers between devices: 42.9 us -> none  [body(): lax.all_to_all(homeward, 'grp', split_axis=0, concat_axis=0, tiled=True)]
    ppermute x0 -> x13, waiting for transfers between devices: none -> 27.2 us  [the longest x8 23.7 us: send(): return lax.ppermute(value, ('z', 'c'), along(shift))]
    ppermute x0 -> x13, starting transfers between devices: none -> 24.7 us  [the longest x8 15.2 us: send(): return lax.ppermute(value, ('z', 'c'), along(shift))]
    reshape x3 -> x0, local copies, waits for them, and re-layouts: 21.1 us -> none  [the longest x2 12.7 us: expert_half(): return half_out.reshape(block_shape)]
    dot_general x2 -> x0, matrix products: 15.3 us -> none  [the longest x1 10.1 us: expert_half(): jnp.dot(hidden, down_half, preferred_element_type=jnp.float32)]
    broadcast_in_dim x3 -> x1, local copies, waits for them, and re-layouts: 12 us -> 0.01 us  [body(): jnp.zeros((block, TAIL - used), BF)]
    pallas_call x0 -> x3, Pallas kernels: none -> 9.15 us  [the longest x1 7.63 us: experts(): pl.pallas_call(expert_kernel, out_shape=jax.ShapeDtypeStruct((count, widt...]
  transfers between devices with their start and end apart: 1 -> 13, of which waited for: 1 -> 8; matrix products, arithmetic and copies ran while one was open for 0% -> 3% of each run, Pallas kernels for 0% -> 1%
where the time goes in v1:
time: 122 us
  blocking collectives  54.6 us (45%)
  waiting for transfers between devices  27.2 us (22%)
  starting transfers between devices  24.7 us (20%)
  Pallas kernels  9.15 us (8%)
  local copies, waits for them, and re-layouts  3.97 us (3%)
  other arithmetic  2.21 us (2%)
    all_to_all x1, blocking collectives, body(): lax.all_to_all(placed.reshape(PLANE, -1, width), ('y', 'x'), 0, 0, tiled=...  29.3 us
    all_to_all x1, blocking collectives, body(): lax.all_to_all(done.reshape(PLANE, -1, width), ('y', 'x'), 0, 0, tiled=True)  25.3 us
    ppermute x8, waiting for transfers between devices, send(): return lax.ppermute(value, ('z', 'c'), along(shift))  23.7 us
    ppermute x8, starting transfers between devices, send(): return lax.ppermute(value, ('z', 'c'), along(shift))  15.2 us
    ppermute x5, starting transfers between devices, swap(): return lax.ppermute(value, 'c', [(0, 1), (1, 0)])  9.5 us
    pallas_call x1, Pallas kernels, experts(): pl.pallas_call(expert_kernel, out_shape=jax.ShapeDtypeStruct((count, widt...  7.63 us
    ppermute x5, waiting for transfers between devices, swap(): return lax.ppermute(value, 'c', [(0, 1), (1, 0)])  3.44 us
    unnamed x5, local copies, waits for them, and re-layouts  2.79 us
  transfers between devices with their start and end apart: 13, of which 8 were waited for; matrix products, arithmetic and copies ran while one was open for 3% of the time, Pallas kernels for 1%

profile of v1, /device:TPU:1, one launch (start us, length us, event | category | flops | bytes accessed | tf_op | source)
XLA Modules:
  0.0 121.8 jit_solution(6942650412426443060)
XLA Ops:
  0.0 3.2 %collective-permute-start.5 = (bf16[3584,512]{1,0:T(8,128)(2,1)}, bf16[3584,512]{1,0:T(8,128)(2,1)}, u32[]{:S(2)}, u32[]{:S(2)}) collective-permute-start(bf16[3584,512]{1,0:T(8,128)(2,1)} %bitcast.10), channel_id=1, source_target_pairs={{0,1},{1,0},{2,3},{3,2},{4,5},{5,4},{6,7},{7,6},{8,9},{9,8},{10,11... | collective-permute-start | bytes 11010056 | tf_op jit(solution)/shard_map/ppermute | solution.py:30
  3.2 0.0 collective-permute-start.6
  3.2 0.5 collective-permute-start.7
  3.8 0.7 reduce_precision.6
  4.4 0.8 copy.11
  5.2 0.7 convert_element_type.35
  5.9 0.1 copy.13
  6.0 0.1 copy.10
  6.1 1.0 concatenate.10.own
  7.1 0.0 copy-start
  7.1 0.1 collective-permute-start
  7.2 2.5 %collective-permute-done = bf16[16,3712]{1,0:T(8,128)(2,1)S(1)} collective-permute-done((bf16[16,3712]{1,0:T(8,128)(2,1)S(1)}, bf16[16,3712]{1,0:T(8,128)(2,1)S(1)}, u32[]{:S(2)}, u32[]{:S(2)}) %collective-permute-start) | collective-permute-done | bytes 118816 | tf_op jit(solution)/shard_map/ppermute | solution.py:30
  9.6 4.4 %collective-permute-start.2 = (bf16[32,3712]{1,0:T(8,128)(2,1)S(1)}, bf16[32,3712]{1,0:T(8,128)(2,1)S(1)}, u32[]{:S(2)}, u32[]{:S(2)}) collective-permute-start(bf16[32,3712]{1,0:T(8,128)(2,1)S(1)} %pad_maximum_fusion), channel_id=1, source_target_pairs={{0,64},{1,193},{32,96},{33,225},{64,128},{65,1},{96,160},{97,33},{... | collective-permute-start | bytes 712712 | tf_op jit(solution)/shard_map/ppermute | solution.py:26
  14.0 0.7 collective-permute-start.1
  14.7 3.7 %collective-permute-done.2.second = bf16[32,3712]{1,0:T(8,128)(2,1)S(1)} collective-permute-done((bf16[32,3712]{1,0:T(8,128)(2,1)S(1)}, bf16[32,3712]{1,0:T(8,128)(2,1)S(1)}, u32[]{:S(2)}, u32[]{:S(2)}) %collective-permute-start.2) | collective-permute-done | bytes 237600 | tf_op jit(solution)/shard_map/ppermute | solution.py:26
  18.5 4.5 %collective-permute-start.3 = (bf16[32,3712]{1,0:T(8,128)(2,1)S(1)}, bf16[32,3712]{1,0:T(8,128)(2,1)S(1)}, u32[]{:S(2)}, u32[]{:S(2)}) collective-permute-start(bf16[32,3712]{1,0:T(8,128)(2,1)S(1)} %collective-permute-done.2.second), channel_id=1, source_target_pairs={{0,32},{1,225},{32,64},{33,1},{64,96},{65,33},{96,128},{97,65},{12... | collective-permute-start | bytes 712712 | tf_op jit(solution)/shard_map/ppermute | solution.py:26
  22.9 0.1 collective-permute-done.1.near
  23.0 1.8 %collective-permute-start.4 = (bf16[16,3712]{1,0:T(8,128)(2,1)S(1)}, bf16[16,3712]{1,0:T(8,128)(2,1)S(1)}, u32[]{:S(2)}, u32[]{:S(2)}) collective-permute-start(bf16[16,3712]{1,0:T(8,128)(2,1)S(1)} %slice.29), channel_id=1, source_target_pairs={{0,64},{1,193},{32,96},{33,225},{64,128},{65,1},{96,160},{97,33},{... | collective-permute-start | bytes 356360 | tf_op jit(solution)/shard_map/ppermute | solution.py:26
  24.8 3.1 %collective-permute-done.4.fourth = bf16[16,3712]{1,0:T(8,128)(2,1)S(1)} collective-permute-done((bf16[16,3712]{1,0:T(8,128)(2,1)S(1)}, bf16[16,3712]{1,0:T(8,128)(2,1)S(1)}, u32[]{:S(2)}, u32[]{:S(2)}) %collective-permute-start.4) | collective-permute-done | bytes 118816 | tf_op jit(solution)/shard_map/ppermute | solution.py:26
  27.9 0.0 collective-permute-done.3.third
  27.9 0.9 place.1
  28.8 29.3 %all_to_all.10 = bf16[16,16,3584]{2,1,0:T(8,128)(2,1)S(1)} all-to-all(bf16[16,16,3584]{2,1,0:T(8,128)(2,1)S(1)} %bitcast.14), channel_id=1, replica_groups=mesh['z'=8,'y'=4,'x'=4,'c'=2] {'y','x'}, dimensions={0} | all-to-all | bytes 3670016 | tf_op jit(solution)/shard_map/all_to_all | solution.py:192
  58.1 0.0 collective-permute-done.5.gate_b
  58.1 0.0 collective-permute-done.6.up_b
  58.1 0.0 collective-permute-done.7.down_b
  58.1 0.0 copy-done
  58.1 0.0 copy-start.1
  58.1 2.0 %copy-done.1 = bf16[1,3584,512]{2,1,0:T(8,128)(2,1)S(1)} copy-done((bf16[1,3584,512]{2,1,0:T(8,128)(2,1)S(1)}, bf16[1,3584,512]{2,1,0:T(8,128)(2,1)}, u32[]{:S(2)}) %copy-start.1) | copy-done | bytes 3670040
  60.1 7.6 %experts.1 = bf16[256,3584]{1,0:T(8,128)(2,1)S(1)} custom-call(bf16[256,3584]{1,0:T(8,128)(2,1)S(1)} %bitcast.7, bf16[3584,512]{1,0:T(8,128)(2,1)S(1)} %bitcast.11, bf16[3584,512]{1,0:T(8,128)(2,1)S(1)} %bitcast.13, bf16[512,3584]{1,0:T(8,128)(2,1)} %bitcast.16, bf16[3584,512]{1,0:T(8,128)(2,1)} %collective-permute-done.5.gate_b, ...), custom_call_target="tpu_custom_call" | custom-call | flops 5637144576 | bytes 25690112 | tf_op jit(solution)/shard_map/experts/pallas_call | solution.py:126
  67.8 25.3 %all_to_all.11 = bf16[16,16,3584]{2,1,0:T(8,128)(2,1)S(1)} all-to-all(bf16[16,16,3584]{2,1,0:T(8,128)(2,1)S(1)} %bitcast.8), channel_id=1, replica_groups=mesh['z'=8,'y'=4,'x'=4,'c'=2] {'y','x'}, dimensions={0} | all-to-all | bytes 3670016 | tf_op jit(solution)/shard_map/all_to_all | solution.py:194
  93.1 0.7 collect.1
  93.7 2.9 %collective-permute-start.9 = (bf16[32,3584]{1,0:T(8,128)(2,1)S(1)}, bf16[32,3584]{1,0:T(8,128)(2,1)S(1)}, u32[]{:S(2)}, u32[]{:S(2)}) collective-permute-start(bf16[32,3584]{1,0:T(8,128)(2,1)S(1)} %get-tuple-element.19), channel_id=1, source_target_pairs={{0,224},{1,33},{32,0},{33,65},{64,32},{65,97},{96,64},{97,129},{12... | collective-permute-start | bytes 688136 | tf_op jit(solution)/shard_map/ppermute | solution.py:26
  96.7 0.7 collective-permute-start.10
  97.4 0.1 collective-permute-start.8
  97.5 9.7 %collective-permute-done.10 = bf16[16,3584]{1,0:T(8,128)(2,1)S(1)} collective-permute-done((bf16[16,3584]{1,0:T(8,128)(2,1)S(1)}, bf16[16,3584]{1,0:T(8,128)(2,1)S(1)}, u32[]{:S(2)}, u32[]{:S(2)}) %collective-permute-start.10) | collective-permute-done | bytes 114720 | tf_op jit(solution)/shard_map/ppermute | solution.py:26
  107.1 0.0 collective-permute-done.9
  107.1 0.1 add_convert_fusion.1
  107.2 0.1 collective-permute-start.11
  107.3 1.1 collective-permute-done.8
  108.4 6.0 %collective-permute-done.11 = bf16[32,3584]{1,0:T(8,128)(2,1)S(1)} collective-permute-done((bf16[32,3584]{1,0:T(8,128)(2,1)S(1)}, bf16[32,3584]{1,0:T(8,128)(2,1)S(1)}, u32[]{:S(2)}, u32[]{:S(2)}) %collective-permute-start.11) | collective-permute-done | bytes 229408 | tf_op jit(solution)/shard_map/ppermute | solution.py:26
  114.5 5.7 %collective-permute-start.12 = (bf16[16,3584]{1,0:T(8,128)(2,1)S(1)}, bf16[16,3584]{1,0:T(8,128)(2,1)S(1)}, u32[]{:S(2)}, u32[]{:S(2)}) collective-permute-start(bf16[16,3584]{1,0:T(8,128)(2,1)S(1)} %slice.44), channel_id=1, source_target_pairs={{0,1},{1,0},{2,3},{3,2},{4,5},{5,4},{6,7},{7,6},{8,9},{9,8},{10,11... | collective-permute-start | bytes 344072 | tf_op jit(solution)/shard_map/ppermute | solution.py:30
  120.2 1.0 collective-permute-done.12
  121.1 0.7 fusion.1
  (7 shorter events, 0.1 us)
Async XLA Ops:
  0.0 58.1 %collective-permute-start.5 = (bf16[3584,512]{1,0:T(8,128)(2,1)}, bf16[3584,512]{1,0:T(8,128)(2,1)}, u32[]{:S(2)}, u32[]{:S(2)}) collective-permute-start(bf16[3584,512]{1,0:T(8,128)(2,1)} %bitcast.10), channel_id=1, source_target_pairs={{0,1},{1,0},{2,3},{3,2},{4,5},{5,4},{6,7},{7,6},{8,9},{9,8},{10,11... | collective-permute-start | bytes 11010056 | tf_op jit(solution)/shard_map/ppermute | solution.py:30
  3.2 54.8 %collective-permute-start.6 = (bf16[3584,512]{1,0:T(8,128)(2,1)}, bf16[3584,512]{1,0:T(8,128)(2,1)}, u32[]{:S(2)}, u32[]{:S(2)}) collective-permute-start(bf16[3584,512]{1,0:T(8,128)(2,1)} %bitcast.12), channel_id=1, source_target_pairs={{0,1},{1,0},{2,3},{3,2},{4,5},{5,4},{6,7},{7,6},{8,9},{9,8},{10,11... | collective-permute-start | bytes 11010056 | tf_op jit(solution)/shard_map/ppermute | solution.py:30
  3.2 54.8 %collective-permute-start.7 = (bf16[512,3584]{1,0:T(8,128)(2,1)}, bf16[512,3584]{1,0:T(8,128)(2,1)}, u32[]{:S(2)}, u32[]{:S(2)}) collective-permute-start(bf16[512,3584]{1,0:T(8,128)(2,1)} %bitcast.15), channel_id=1, source_target_pairs={{0,1},{1,0},{2,3},{3,2},{4,5},{5,4},{6,7},{7,6},{8,9},{9,8},{10,11... | collective-permute-start | bytes 11010056 | tf_op jit(solution)/shard_map/ppermute | solution.py:30
  7.1 51.0 %copy-start = (bf16[1,3584,512]{2,1,0:T(8,128)(2,1)S(1)}, bf16[1,3584,512]{2,1,0:T(8,128)(2,1)}, u32[]{:S(2)}) copy-start(bf16[1,3584,512]{2,1,0:T(8,128)(2,1)} %param.9) | copy-start | bytes 11010052
  7.1 2.6 %collective-permute-start = (bf16[16,3712]{1,0:T(8,128)(2,1)S(1)}, bf16[16,3712]{1,0:T(8,128)(2,1)S(1)}, u32[]{:S(2)}, u32[]{:S(2)}) collective-permute-start(bf16[16,3712]{1,0:T(8,128)(2,1)S(1)} %concatenate.10.own), channel_id=1, source_target_pairs={{0,1},{1,0},{2,3},{3,2},{4,5},{5,4},{6,7},{7,6},{8,9},{9,8},{10,11... | collective-permute-start | bytes 356360 | tf_op jit(solution)/shard_map/ppermute | solution.py:30
  9.6 8.8 %collective-permute-start.2 = (bf16[32,3712]{1,0:T(8,128)(2,1)S(1)}, bf16[32,3712]{1,0:T(8,128)(2,1)S(1)}, u32[]{:S(2)}, u32[]{:S(2)}) collective-permute-start(bf16[32,3712]{1,0:T(8,128)(2,1)S(1)} %pad_maximum_fusion), channel_id=1, source_target_pairs={{0,64},{1,193},{32,96},{33,225},{64,128},{65,1},{96,160},{97,33},{... | collective-permute-start | bytes 712712 | tf_op jit(solution)/shard_map/ppermute | solution.py:26
  14.0 9.0 %collective-permute-start.1 = (bf16[32,3712]{1,0:T(8,128)(2,1)S(1)}, bf16[32,3712]{1,0:T(8,128)(2,1)S(1)}, u32[]{:S(2)}, u32[]{:S(2)}) collective-permute-start(bf16[32,3712]{1,0:T(8,128)(2,1)S(1)} %pad_maximum_fusion), channel_id=1, source_target_pairs={{0,32},{1,225},{32,64},{33,1},{64,96},{65,33},{96,128},{97,65},{12... | collective-permute-start | bytes 712712 | tf_op jit(solution)/shard_map/ppermute | solution.py:26
  18.5 9.5 %collective-permute-start.3 = (bf16[32,3712]{1,0:T(8,128)(2,1)S(1)}, bf16[32,3712]{1,0:T(8,128)(2,1)S(1)}, u32[]{:S(2)}, u32[]{:S(2)}) collective-permute-start(bf16[32,3712]{1,0:T(8,128)(2,1)S(1)} %collective-permute-done.2.second), channel_id=1, source_target_pairs={{0,32},{1,225},{32,64},{33,1},{64,96},{65,33},{96,128},{97,65},{12... | collective-permute-start | bytes 712712 | tf_op jit(solution)/shard_map/ppermute | solution.py:26
  23.0 4.9 %collective-permute-start.4 = (bf16[16,3712]{1,0:T(8,128)(2,1)S(1)}, bf16[16,3712]{1,0:T(8,128)(2,1)S(1)}, u32[]{:S(2)}, u32[]{:S(2)}) collective-permute-start(bf16[16,3712]{1,0:T(8,128)(2,1)S(1)} %slice.29), channel_id=1, source_target_pairs={{0,64},{1,193},{32,96},{33,225},{64,128},{65,1},{96,160},{97,33},{... | collective-permute-start | bytes 356360 | tf_op jit(solution)/shard_map/ppermute | solution.py:26
  58.1 2.0 %copy-start.1 = (bf16[1,3584,512]{2,1,0:T(8,128)(2,1)S(1)}, bf16[1,3584,512]{2,1,0:T(8,128)(2,1)}, u32[]{:S(2)}) copy-start(bf16[1,3584,512]{2,1,0:T(8,128)(2,1)} %param.10) | copy-start | bytes 11010052
  93.7 13.4 %collective-permute-start.9 = (bf16[32,3584]{1,0:T(8,128)(2,1)S(1)}, bf16[32,3584]{1,0:T(8,128)(2,1)S(1)}, u32[]{:S(2)}, u32[]{:S(2)}) collective-permute-start(bf16[32,3584]{1,0:T(8,128)(2,1)S(1)} %get-tuple-element.19), channel_id=1, source_target_pairs={{0,224},{1,33},{32,0},{33,65},{64,32},{65,97},{96,64},{97,129},{12... | collective-permute-start | bytes 688136 | tf_op jit(solution)/shard_map/ppermute | solution.py:26
  96.7 10.5 %collective-permute-start.10 = (bf16[16,3584]{1,0:T(8,128)(2,1)S(1)}, bf16[16,3584]{1,0:T(8,128)(2,1)S(1)}, u32[]{:S(2)}, u32[]{:S(2)}) collective-permute-start(bf16[16,3584]{1,0:T(8,128)(2,1)S(1)} %get-tuple-element.20), channel_id=1, source_target_pairs={{0,192},{1,65},{32,224},{33,97},{64,0},{65,129},{96,32},{97,161},{... | collective-permute-start | bytes 344072 | tf_op jit(solution)/shard_map/ppermute | solution.py:26
  97.4 11.1 %collective-permute-start.8 = (bf16[32,3584]{1,0:T(8,128)(2,1)S(1)}, bf16[32,3584]{1,0:T(8,128)(2,1)S(1)}, u32[]{:S(2)}, u32[]{:S(2)}) collective-permute-start(bf16[32,3584]{1,0:T(8,128)(2,1)S(1)} %get-tuple-element.17), channel_id=1, source_target_pairs={{0,224},{1,33},{32,0},{33,65},{64,32},{65,97},{96,64},{97,129},{12... | collective-permute-start | bytes 688136 | tf_op jit(solution)/shard_map/ppermute | solution.py:26
  107.2 7.2 %collective-permute-start.11 = (bf16[32,3584]{1,0:T(8,128)(2,1)S(1)}, bf16[32,3584]{1,0:T(8,128)(2,1)S(1)}, u32[]{:S(2)}, u32[]{:S(2)}) collective-permute-start(bf16[32,3584]{1,0:T(8,128)(2,1)S(1)} %pad_maximum_fusion.1), channel_id=1, source_target_pairs={{0,192},{1,65},{32,224},{33,97},{64,0},{65,129},{96,32},{97,161},{... | collective-permute-start | bytes 688136 | tf_op jit(solution)/shard_map/ppermute | solution.py:26
  114.5 6.6 %collective-permute-start.12 = (bf16[16,3584]{1,0:T(8,128)(2,1)S(1)}, bf16[16,3584]{1,0:T(8,128)(2,1)S(1)}, u32[]{:S(2)}, u32[]{:S(2)}) collective-permute-start(bf16[16,3584]{1,0:T(8,128)(2,1)S(1)} %slice.44), channel_id=1, source_target_pairs={{0,1},{1,0},{2,3},{3,2},{4,5},{5,4},{6,7},{7,6},{8,9},{9,8},{10,11... | collective-permute-start | bytes 344072 | tf_op jit(solution)/shard_map/ppermute | solution.py:30

commit v2 on v1

v2 whole, which is shorter than its diff:
```python
import jax
import jax.numpy as jnp
from jax import lax
from jax.experimental import pallas as pl
from jax.experimental.pallas import tpu as pltpu
from jax.sharding import Mesh, PartitionSpec as P

Z, Y, X, C = 8, 4, 4, 2
PLANE = Y * X
SLOTS = 2
TAIL = 128
BF = jnp.bfloat16
F32 = jnp.float32
MIB = 1 << 20
VMEM = pl.BlockSpec(memory_space=pltpu.VMEM)


def along(shift):
    pairs = []
    for z in range(Z):
        pairs.append((z * C, (z + shift) % Z * C))
        pairs.append((z * C + 1, (z - shift) % Z * C + 1))
    return pairs


def across(shift):
    pairs = []
    for z in range(Z):
        pairs.append((z * C, (z - shift) % Z * C + 1))
        pairs.append((z * C + 1, (z + shift) % Z * C))
    return pairs


def send(value, shift):
    return lax.ppermute(value, ("z", "c"), along(shift))


def back_across(value, shift):
    return lax.ppermute(value, ("z", "c"), across(shift))


def swap(value):
    return lax.ppermute(value, "c", [(0, 1), (1, 0)])


def extend_kernel(tokens, ids, gates, out):
    block, width = tokens.shape
    gate = gates[...]
    high = gate.astype(BF)
    rest = gate - high.astype(F32)
    middle = rest.astype(BF)
    low = (rest - middle.astype(F32)).astype(BF)
    parts = [v.astype(F32) for v in (ids[...], high, middle, low)]
    used = sum(p.shape[0] for p in parts)
    parts.append(jnp.zeros((TAIL - used, block), F32))
    table = jnp.concatenate(parts, axis=0).astype(BF)
    left = lax.broadcasted_iota(jnp.int32, (block, block), 0)
    right = lax.broadcasted_iota(jnp.int32, (block, block), 1)
    unit = jnp.where(left == right, 1.0, 0.0).astype(BF)
    tail = lax.dot_general(unit, table, (((1,), (1,)), ((), ())), preferred_element_type=F32)
    out[:, :width] = tokens[...]
    out[:, width:] = tail.astype(BF)


def extend(tokens, expert_ids, gates):
    block, width = tokens.shape
    return pl.pallas_call(
        extend_kernel,
        out_shape=jax.ShapeDtypeStruct((block, width + TAIL), BF),
        name="extend",
    )(tokens, expert_ids.T, gates.T)


def place_kernel(block, *refs):
    pieces, (rows_out, high_out, low_out) = list(refs[:-3]), refs[-3:]
    pieces[0] = pieces[0].at[:block]
    width = rows_out.shape[1]
    rows = sum(p.shape[0] for p in pieces)
    blocks = rows // block
    per_expert = blocks * SLOTS
    slots = PLANE * per_expert
    tail = [p[:, width:].astype(F32) for p in pieces]
    if rows < TAIL:
        tail.append(jnp.zeros((TAIL - rows, TAIL), F32))
    tail = jnp.concatenate(tail, axis=0).T[:, :rows]
    expert = (lax.axis_index("z") * PLANE + lax.broadcasted_iota(jnp.int32, (PLANE, rows), 0)).astype(F32)
    named = jnp.zeros((PLANE, rows), F32)
    gate = jnp.zeros((PLANE, rows), F32)
    for k in range(8):
        hit = tail[k : k + 1] == expert
        value = tail[8 + k : 9 + k] + tail[16 + k : 17 + k] + tail[24 + k : 25 + k]
        named = named + jnp.where(hit, 1.0, 0.0)
        gate = gate + jnp.where(hit, value, 0.0)
    before = lax.broadcasted_iota(jnp.int32, (rows, rows), 0)
    after = lax.broadcasted_iota(jnp.int32, (rows, rows), 1)
    earlier = jnp.where((before < after) & (before // block == after // block), 1.0, 0.0).astype(BF)
    rank = jnp.dot(named.astype(BF), earlier, preferred_element_type=F32)

    def spread(value):
        return jnp.broadcast_to(value[:, None, :], (PLANE, per_expert, rows)).reshape(slots, rows)

    slot = lax.broadcasted_iota(jnp.int32, (slots, rows), 0)
    lane = lax.broadcasted_iota(jnp.int32, (slots, rows), 1)
    here = (slot // SLOTS) % blocks == lane // block
    chosen = here & (spread(named) > 0.5) & (spread(rank) == (slot % SLOTS).astype(F32))
    weight = jnp.where(chosen, spread(gate), 0.0)
    high = weight.astype(BF)
    high_out[...] = high
    low_out[...] = (weight - high.astype(F32)).astype(BF)
    pick = jnp.where(chosen, 1.0, 0.0).astype(BF)
    step = 512
    for c in range(0, width, step):
        part = jnp.concatenate([p[:, c : c + step] for p in pieces], axis=0)
        rows_out[:, c : c + step] = jnp.dot(pick, part, preferred_element_type=F32).astype(BF)


def place(pieces, block, width):
    rows = sum(p.shape[0] for p in pieces) - block
    slots = PLANE * SLOTS * (rows // block)

    def kernel(*refs):
        place_kernel(block, *refs)

    return pl.pallas_call(
        kernel,
        out_shape=(
            jax.ShapeDtypeStruct((slots, width), BF),
            jax.ShapeDtypeStruct((slots, rows), BF),
            jax.ShapeDtypeStruct((slots, rows), BF),
        ),
        compiler_params=pltpu.CompilerParams(vmem_limit_bytes=16 * MIB),
        cost_estimate=pl.CostEstimate(flops=2 * slots * rows * width, bytes_accessed=2 * (slots + rows) * width, transcendentals=0),
        name="place",
    )(*pieces)


def expert_kernel(rows, gate_a, up_a, down_a, gate_b, up_b, down_b, out, gate_v, up_v, down_v, hidden, sems):
    half = gate_a.shape[1]
    width = out.shape[1]
    pairs = ((gate_a, gate_v), (up_a, up_v), (down_a, down_v))
    copies = [pltpu.make_async_copy(src, dst, sems.at[i]) for i, (src, dst) in enumerate(pairs)]
    for copy in copies:
        copy.start()
    tile = 256
    for h, (gate, up) in enumerate(((gate_b, up_b), (gate_v, up_v))):
        if h == 1:
            copies[0].wait()
            copies[1].wait()
        for j in range(0, half, tile):
            g = jnp.dot(rows[...], gate[:, j : j + tile], preferred_element_type=F32)
            u = jnp.dot(rows[...], up[:, j : j + tile], preferred_element_type=F32)
            hidden[:, h * half + j : h * half + j + tile] = (g / (1.0 + jnp.exp(-g)) * u).astype(BF)
    copies[2].wait()
    for c in range(0, width, tile):
        total = jnp.dot(hidden[:, :half], down_b[:, c : c + tile], preferred_element_type=F32)
        total = total + jnp.dot(hidden[:, half:], down_v[:, c : c + tile], preferred_element_type=F32)
        out[:, c : c + tile] = total.astype(BF)


def experts(rows, own, other):
    width, half = own[0].shape
    count = rows.shape[0]
    return pl.pallas_call(
        expert_kernel,
        out_shape=jax.ShapeDtypeStruct(rows.shape, BF),
        in_specs=[VMEM] + [pl.BlockSpec(memory_space=pl.ANY)] * 3 + [VMEM] * 3,
        out_specs=VMEM,
        scratch_shapes=[
            pltpu.VMEM((width, half), BF),
            pltpu.VMEM((width, half), BF),
            pltpu.VMEM((half, width), BF),
            pltpu.VMEM((count, 2 * half), BF),
            pltpu.SemaphoreType.DMA((3,)),
        ],
        compiler_params=pltpu.CompilerParams(vmem_limit_bytes=32 * MIB),
        cost_estimate=pl.CostEstimate(
            flops=2 * count * width * half * 6, bytes_accessed=12 * width * half + 4 * count * width, transcendentals=2 * count * half
        ),
        name="experts",
    )(rows, *own, *other)


def collect_kernel(returned, high, low, *outs):
    step = 512
    over = (((0,), (0,)), ((), ()))
    for c in range(0, returned.shape[1], step):
        part = returned[:, c : c + step]
        total = lax.dot_general(high[...], part, over, preferred_element_type=F32)
        total = total + lax.dot_general(low[...], part, over, preferred_element_type=F32)
        start = 0
        for out in outs:
            count = out.shape[0]
            out[:, c : c + step] = total[start : start + count].astype(out.dtype)
            start += count


def collect(returned, high, low, shapes):
    slots, width = returned.shape
    rows = high.shape[1]
    return pl.pallas_call(
        collect_kernel,
        out_shape=[jax.ShapeDtypeStruct((count, width), kind) for count, kind in shapes],
        compiler_params=pltpu.CompilerParams(vmem_limit_bytes=16 * MIB),
        cost_estimate=pl.CostEstimate(flops=4 * slots * rows * width, bytes_accessed=2 * (slots + rows) * width, transcendentals=0),
        name="collect",
    )(returned, high, low)


def exchange(value):
    width = value.shape[1]
    return lax.all_to_all(value.reshape(PLANE, -1, width), ("y", "x"), 0, 0, tiled=True).reshape(-1, width)


def body(tokens, expert_ids, gates, gate_weight, up_weight, down_weight):
    block, width = tokens.shape
    own_weights = [gate_weight[0], up_weight[0], down_weight[0]]
    own = extend(tokens, expert_ids, gates)
    other, sent_weights = lax.optimization_barrier((swap(own), own_weights))
    other_weights = [swap(w) for w in sent_weights]
    own_weights = [pltpu.with_memory_space_constraint(w, pltpu.HBM) for w in own_weights]
    other_weights = [pltpu.with_memory_space_constraint(w, pltpu.VMEM) for w in other_weights]

    both = jnp.concatenate([own, other], axis=0)
    second = send(both, 2)
    near = send(both, 1)
    third = send(second, 1)
    fourth = send(second[:block], 2)
    rows, high, low = place((both, near, second, third, fourth), block, width)
    done = experts(exchange(rows), own_weights, other_weights)
    returned = exchange(done)
    shapes = ((block, F32), (block, BF), (block, BF), (block, F32), (block, F32), (2 * block, BF), (block, BF))
    q_own, q_near, q_near_other, q_second, q_second_other, q_third, q_fourth = collect(returned, high, low, shapes)
    third = send(q_third, -1)
    fourth = send(q_fourth, -2)
    near = send(q_near, -1)
    near_other = back_across(q_near_other, 1)
    second = send((q_second + third[:block].astype(F32) + fourth.astype(F32)).astype(BF), -2)
    second_other = back_across((q_second_other + third[block:].astype(F32)).astype(BF), 2)
    total = q_own + near.astype(F32) + near_other.astype(F32)
    return (total + second.astype(F32) + second_other.astype(F32)).astype(BF)


def solution(mesh):
    fine = Mesh(mesh.devices.reshape(Z, Y, X, C), ("z", "y", "x", "c"))
    rows = P(("z", "y", "x", "c"))
    return jax.shard_map(body, mesh=fine, in_specs=(rows,) * 6, out_specs=rows, check_vma=False)
```

time: 122 us -> 116 us (0.951)
  waiting for transfers between devices: 27.2 us -> 15 us
  starting transfers between devices: 24.7 us -> 32 us
  local copies, waits for them, and re-layouts: 3.97 us -> 0.01 us
  Pallas kernels: 9.15 us -> 10.6 us
    ppermute x8, waiting for transfers between devices: 23.7 us -> 9.12 us  [send(): return lax.ppermute(value, ('z', 'c'), along(shift))]
    ppermute x0 -> x2, starting transfers between devices: none -> 12 us  [back_across(): return lax.ppermute(value, ('z', 'c'), across(shift))]
    ppermute x5 -> x4, starting transfers between devices: 9.5 us -> 4.11 us  [swap(): return lax.ppermute(value, 'c', [(0, 1), (1, 0)])]
    ppermute x0 -> x2, waiting for transfers between devices: none -> 4.72 us  [back_across(): return lax.ppermute(value, ('z', 'c'), across(shift))]
    unnamed x5 -> x0, local copies, waits for them, and re-layouts: 2.79 us -> none
    ppermute x5 -> x4, waiting for transfers between devices: 3.44 us -> 1.19 us  [swap(): return lax.ppermute(value, 'c', [(0, 1), (1, 0)])]
    pallas_call x3 -> x4, Pallas kernels: 9.15 us -> 10.6 us  [the longest x1 7.33 us: experts(): pl.pallas_call(expert_kernel, out_shape=jax.ShapeDtypeStruct(rows.shape,...]
  transfers between devices with their start and end apart: 13 -> 14, of which waited for: 8 -> 7; matrix products, arithmetic and copies ran while one was open for 3% -> 1% of each run, Pallas kernels for 1% -> 1%
where the time goes in v2:
time: 116 us; the launch traced here: 115 us
  blocking collectives  55.5 us (48%)
  starting transfers between devices  32 us (28%)
  waiting for transfers between devices  15 us (13%)
  Pallas kernels  10.6 us (9%)
  other arithmetic  1.71 us (1%)
    all_to_all x2, blocking collectives, exchange(): lax.all_to_all(value.reshape(PLANE, -1, width), ('y', 'x'), 0, 0, tiled=T...  55.5 us
    ppermute x8, starting transfers between devices, send(): return lax.ppermute(value, ('z', 'c'), along(shift))  15.8 us
    ppermute x2, starting transfers between devices, back_across(): return lax.ppermute(value, ('z', 'c'), across(shift))  12 us
    ppermute x8, waiting for transfers between devices, send(): return lax.ppermute(value, ('z', 'c'), along(shift))  9.12 us
    pallas_call x1, Pallas kernels, experts(): pl.pallas_call(expert_kernel, out_shape=jax.ShapeDtypeStruct(rows.shape,...  7.33 us
    ppermute x2, waiting for transfers between devices, back_across(): return lax.ppermute(value, ('z', 'c'), across(shift))  4.72 us
    ppermute x4, starting transfers between devices, swap(): return lax.ppermute(value, 'c', [(0, 1), (1, 0)])  4.11 us
  transfers between devices with their start and end apart: 14, of which 7 were waited for; matrix products, arithmetic and copies ran while one was open for 1% of the time, Pallas kernels for 1%

profile of v2, /device:TPU:1, one launch (start us, length us, event | category | flops | bytes accessed | tf_op | source)
XLA Modules:
  0.0 114.8 jit_solution(12462105241401775996)
XLA Ops:
  0.0 1.7 %extend.1 = bf16[16,3712]{1,0:T(8,128)(2,1)} custom-call(bf16[16,3584]{1,0:T(8,128)(2,1)} %tokens.1, s32[8,16]{1,0:T(8,128)} %bitcast.19, f32[8,16]{1,0:T(8,128)} %bitcast.20), custom_call_target="tpu_custom_call" | custom-call | tf_op jit(solution)/shard_map/extend/pallas_call | solution.py:67
  1.7 3.2 %collective-permute-start = (bf16[16,3712]{1,0:T(8,128)(2,1)}, bf16[16,3712]{1,0:T(8,128)(2,1)S(1)}, u32[]{:S(2)}, u32[]{:S(2)}) collective-permute-start(bf16[16,3712]{1,0:T(8,128)(2,1)} %extend.1), channel_id=1, source_target_pairs={{0,1},{1,0},{2,3},{3,2},{4,5},{5,4},{6,7},{7,6},{8,9},{9,8},{10,11... | collective-permute-start | bytes 356360 | tf_op jit(solution)/shard_map/ppermute | solution.py:43
  4.9 1.2 %collective-permute-done = bf16[16,3712]{1,0:T(8,128)(2,1)S(1)} collective-permute-done((bf16[16,3712]{1,0:T(8,128)(2,1)}, bf16[16,3712]{1,0:T(8,128)(2,1)S(1)}, u32[]{:S(2)}, u32[]{:S(2)}) %collective-permute-start) | collective-permute-done | bytes 118816 | tf_op jit(solution)/shard_map/ppermute | solution.py:43
  6.1 0.4 collective-permute-start.5
  6.5 0.2 collective-permute-start.6
  6.6 0.4 collective-permute-start.7
  7.0 0.9 pad_maximum_fusion.refs_0_
  7.9 4.4 %collective-permute-start.2 = (bf16[32,3712]{1,0:T(8,128)(2,1)S(1)}, bf16[32,3712]{1,0:T(8,128)(2,1)S(1)}, u32[]{:S(2)}, u32[]{:S(2)}) collective-permute-start(bf16[32,3712]{1,0:T(8,128)(2,1)S(1)} %pad_maximum_fusion.refs_0_), channel_id=1, source_target_pairs={{0,64},{1,193},{32,96},{33,225},{64,128},{65,1},{96,160},{97,33},{... | collective-permute-start | bytes 712712 | tf_op jit(solution)/shard_map/ppermute | solution.py:35
  12.3 0.7 collective-permute-start.1
  13.0 3.7 %collective-permute-done.2.refs_2_ = bf16[32,3712]{1,0:T(8,128)(2,1)S(1)} collective-permute-done((bf16[32,3712]{1,0:T(8,128)(2,1)S(1)}, bf16[32,3712]{1,0:T(8,128)(2,1)S(1)}, u32[]{:S(2)}, u32[]{:S(2)}) %collective-permute-start.2) | collective-permute-done | bytes 237600 | tf_op jit(solution)/shard_map/ppermute | solution.py:35
  16.7 4.5 %collective-permute-start.3 = (bf16[32,3712]{1,0:T(8,128)(2,1)S(1)}, bf16[32,3712]{1,0:T(8,128)(2,1)S(1)}, u32[]{:S(2)}, u32[]{:S(2)}) collective-permute-start(bf16[32,3712]{1,0:T(8,128)(2,1)S(1)} %collective-permute-done.2.refs_2_), channel_id=1, source_target_pairs={{0,32},{1,225},{32,64},{33,1},{64,96},{65,33},{96,128},{97,65},{12... | collective-permute-start | bytes 712712 | tf_op jit(solution)/shard_map/ppermute | solution.py:35
  21.2 0.1 collective-permute-done.1.refs_1_
  21.3 1.8 %collective-permute-start.4 = (bf16[16,3712]{1,0:T(8,128)(2,1)S(1)}, bf16[16,3712]{1,0:T(8,128)(2,1)S(1)}, u32[]{:S(2)}, u32[]{:S(2)}) collective-permute-start(bf16[16,3712]{1,0:T(8,128)(2,1)S(1)} %slice.12), channel_id=1, source_target_pairs={{0,64},{1,193},{32,96},{33,225},{64,128},{65,1},{96,160},{97,33},{... | collective-permute-start | bytes 356360 | tf_op jit(solution)/shard_map/ppermute | solution.py:35
  23.1 3.1 %collective-permute-done.4.refs_4_ = bf16[16,3712]{1,0:T(8,128)(2,1)S(1)} collective-permute-done((bf16[16,3712]{1,0:T(8,128)(2,1)S(1)}, bf16[16,3712]{1,0:T(8,128)(2,1)S(1)}, u32[]{:S(2)}, u32[]{:S(2)}) %collective-permute-start.4) | collective-permute-done | bytes 118816 | tf_op jit(solution)/shard_map/ppermute | solution.py:35
  26.2 0.0 collective-permute-done.3.refs_3_
  26.2 0.9 place.1
  27.1 29.4 %all_to_all.10 = bf16[16,16,3584]{2,1,0:T(8,128)(2,1)S(1)} all-to-all(bf16[16,16,3584]{2,1,0:T(8,128)(2,1)S(1)} %bitcast.12), channel_id=1, replica_groups=mesh['z'=8,'y'=4,'x'=4,'c'=2] {'y','x'}, dimensions={0} | all-to-all | bytes 3670016 | tf_op jit(solution)/shard_map/all_to_all | solution.py:211
  56.5 0.0 collective-permute-done.5.gate_b
  56.5 0.0 collective-permute-done.6.up_b
  56.5 0.0 collective-permute-done.7.down_b
  56.5 7.3 %experts.1 = bf16[256,3584]{1,0:T(8,128)(2,1)S(1)} custom-call(bf16[256,3584]{1,0:T(8,128)(2,1)S(1)} %bitcast.9, bf16[3584,512]{1,0:T(8,128)(2,1)} %bitcast.14, bf16[3584,512]{1,0:T(8,128)(2,1)} %bitcast.16, bf16[512,3584]{1,0:T(8,128)(2,1)} %bitcast.18, bf16[3584,512]{1,0:T(8,128)(2,1)S(1)} %collective-permute-done.5.gate_b, ...), custom_call_target="tpu_custom_call" | custom-call | flops 5637144576 | bytes 25690112 | tf_op jit(solution)/shard_map/experts/pallas_call | solution.py:163
  63.8 26.0 %all_to_all.11 = bf16[16,16,3584]{2,1,0:T(8,128)(2,1)S(1)} all-to-all(bf16[16,16,3584]{2,1,0:T(8,128)(2,1)S(1)} %bitcast.10), channel_id=1, replica_groups=mesh['z'=8,'y'=4,'x'=4,'c'=2] {'y','x'}, dimensions={0} | all-to-all | bytes 3670016 | tf_op jit(solution)/shard_map/all_to_all | solution.py:211
  89.9 0.7 collect.1
  90.6 2.7 %collective-permute-start.10 = (bf16[32,3584]{1,0:T(8,128)(2,1)S(1)}, bf16[32,3584]{1,0:T(8,128)(2,1)S(1)}, u32[]{:S(2)}, u32[]{:S(2)}) collective-permute-start(bf16[32,3584]{1,0:T(8,128)(2,1)S(1)} %get-tuple-element.30), channel_id=1, source_target_pairs={{0,224},{1,33},{32,0},{33,65},{64,32},{65,97},{96,64},{97,129},{12... | collective-permute-start | bytes 688136 | tf_op jit(solution)/shard_map/ppermute | solution.py:35
  93.3 0.5 collective-permute-start.11
  93.7 0.3 collective-permute-start.8
  94.0 7.8 %collective-permute-start.9 = (bf16[16,3584]{1,0:T(8,128)(2,1)S(1)}, bf16[16,3584]{1,0:T(8,128)(2,1)S(1)}, u32[]{:S(2)}, u32[]{:S(2)}) collective-permute-start(bf16[16,3584]{1,0:T(8,128)(2,1)S(1)} %get-tuple-element.28), channel_id=1, source_target_pairs={{0,225},{1,32},{32,1},{33,64},{64,33},{65,96},{96,65},{97,128},{12... | collective-permute-start | bytes 344072 | tf_op jit(solution)/shard_map/ppermute | solution.py:39
  101.8 1.7 %collective-permute-done.11 = bf16[16,3584]{1,0:T(8,128)(2,1)S(1)} collective-permute-done((bf16[16,3584]{1,0:T(8,128)(2,1)S(1)}, bf16[16,3584]{1,0:T(8,128)(2,1)S(1)}, u32[]{:S(2)}, u32[]{:S(2)}) %collective-permute-start.11) | collective-permute-done | bytes 114720 | tf_op jit(solution)/shard_map/ppermute | solution.py:35
  103.5 0.0 collective-permute-done.10
  103.5 0.1 add_convert_fusion.2
  103.5 1.0 collective-permute-start.12
  104.6 4.2 %collective-permute-start.13 = (bf16[16,3584]{1,0:T(8,128)(2,1)S(1)}, bf16[16,3584]{1,0:T(8,128)(2,1)S(1)}, u32[]{:S(2)}, u32[]{:S(2)}) collective-permute-start(bf16[16,3584]{1,0:T(8,128)(2,1)S(1)} %get-tuple-element.34), channel_id=1, source_target_pairs={{0,193},{1,64},{32,225},{33,96},{64,1},{65,128},{96,33},{97,160},{... | collective-permute-start | bytes 344072 | tf_op jit(solution)/shard_map/ppermute | solution.py:39
  108.8 0.0 collective-permute-done.8
  108.8 0.0 collective-permute-done.9
  108.8 0.5 collective-permute-done.12
  109.4 4.7 %collective-permute-done.13 = bf16[16,3584]{1,0:T(8,128)(2,1)S(1)} collective-permute-done((bf16[16,3584]{1,0:T(8,128)(2,1)S(1)}, bf16[16,3584]{1,0:T(8,128)(2,1)S(1)}, u32[]{:S(2)}, u32[]{:S(2)}) %collective-permute-start.13) | collective-permute-done | bytes 114720 | tf_op jit(solution)/shard_map/ppermute | solution.py:39
  114.1 0.7 add_convert_fusion
  (1 shorter events, 0.0 us)
Async XLA Ops:
  1.7 4.4 %collective-permute-start = (bf16[16,3712]{1,0:T(8,128)(2,1)}, bf16[16,3712]{1,0:T(8,128)(2,1)S(1)}, u32[]{:S(2)}, u32[]{:S(2)}) collective-permute-start(bf16[16,3712]{1,0:T(8,128)(2,1)} %extend.1), channel_id=1, source_target_pairs={{0,1},{1,0},{2,3},{3,2},{4,5},{5,4},{6,7},{7,6},{8,9},{9,8},{10,11... | collective-permute-start | bytes 356360 | tf_op jit(solution)/shard_map/ppermute | solution.py:43
  6.1 50.4 %collective-permute-start.5 = (bf16[3584,512]{1,0:T(8,128)(2,1)}, bf16[3584,512]{1,0:T(8,128)(2,1)S(1)}, u32[]{:S(2)}, u32[]{:S(2)}) collective-permute-start(bf16[3584,512]{1,0:T(8,128)(2,1)} %bitcast.13), channel_id=1, source_target_pairs={{0,1},{1,0},{2,3},{3,2},{4,5},{5,4},{6,7},{7,6},{8,9},{9,8},{10,11... | collective-permute-start | bytes 11010056 | tf_op jit(solution)/shard_map/ppermute | solution.py:43
  6.5 50.0 %collective-permute-start.6 = (bf16[3584,512]{1,0:T(8,128)(2,1)}, bf16[3584,512]{1,0:T(8,128)(2,1)S(1)}, u32[]{:S(2)}, u32[]{:S(2)}) collective-permute-start(bf16[3584,512]{1,0:T(8,128)(2,1)} %bitcast.15), channel_id=1, source_target_pairs={{0,1},{1,0},{2,3},{3,2},{4,5},{5,4},{6,7},{7,6},{8,9},{9,8},{10,11... | collective-permute-start | bytes 11010056 | tf_op jit(solution)/shard_map/ppermute | solution.py:43
  6.6 49.9 %collective-permute-start.7 = (bf16[512,3584]{1,0:T(8,128)(2,1)}, bf16[512,3584]{1,0:T(8,128)(2,1)S(1)}, u32[]{:S(2)}, u32[]{:S(2)}) collective-permute-start(bf16[512,3584]{1,0:T(8,128)(2,1)} %bitcast.17), channel_id=1, source_target_pairs={{0,1},{1,0},{2,3},{3,2},{4,5},{5,4},{6,7},{7,6},{8,9},{9,8},{10,11... | collective-permute-start | bytes 11010056 | tf_op jit(solution)/shard_map/ppermute | solution.py:43
  7.9 8.8 %collective-permute-start.2 = (bf16[32,3712]{1,0:T(8,128)(2,1)S(1)}, bf16[32,3712]{1,0:T(8,128)(2,1)S(1)}, u32[]{:S(2)}, u32[]{:S(2)}) collective-permute-start(bf16[32,3712]{1,0:T(8,128)(2,1)S(1)} %pad_maximum_fusion.refs_0_), channel_id=1, source_target_pairs={{0,64},{1,193},{32,96},{33,225},{64,128},{65,1},{96,160},{97,33},{... | collective-permute-start | bytes 712712 | tf_op jit(solution)/shard_map/ppermute | solution.py:35
  12.3 9.0 %collective-permute-start.1 = (bf16[32,3712]{1,0:T(8,128)(2,1)S(1)}, bf16[32,3712]{1,0:T(8,128)(2,1)S(1)}, u32[]{:S(2)}, u32[]{:S(2)}) collective-permute-start(bf16[32,3712]{1,0:T(8,128)(2,1)S(1)} %pad_maximum_fusion.refs_0_), channel_id=1, source_target_pairs={{0,32},{1,225},{32,64},{33,1},{64,96},{65,33},{96,128},{97,65},{12... | collective-permute-start | bytes 712712 | tf_op jit(solution)/shard_map/ppermute | solution.py:35
  16.7 9.5 %collective-permute-start.3 = (bf16[32,3712]{1,0:T(8,128)(2,1)S(1)}, bf16[32,3712]{1,0:T(8,128)(2,1)S(1)}, u32[]{:S(2)}, u32[]{:S(2)}) collective-permute-start(bf16[32,3712]{1,0:T(8,128)(2,1)S(1)} %collective-permute-done.2.refs_2_), channel_id=1, source_target_pairs={{0,32},{1,225},{32,64},{33,1},{64,96},{65,33},{96,128},{97,65},{12... | collective-permute-start | bytes 712712 | tf_op jit(solution)/shard_map/ppermute | solution.py:35
  21.3 4.9 %collective-permute-start.4 = (bf16[16,3712]{1,0:T(8,128)(2,1)S(1)}, bf16[16,3712]{1,0:T(8,128)(2,1)S(1)}, u32[]{:S(2)}, u32[]{:S(2)}) collective-permute-start(bf16[16,3712]{1,0:T(8,128)(2,1)S(1)} %slice.12), channel_id=1, source_target_pairs={{0,64},{1,193},{32,96},{33,225},{64,128},{65,1},{96,160},{97,33},{... | collective-permute-start | bytes 356360 | tf_op jit(solution)/shard_map/ppermute | solution.py:35
  90.6 12.9 %collective-permute-start.10 = (bf16[32,3584]{1,0:T(8,128)(2,1)S(1)}, bf16[32,3584]{1,0:T(8,128)(2,1)S(1)}, u32[]{:S(2)}, u32[]{:S(2)}) collective-permute-start(bf16[32,3584]{1,0:T(8,128)(2,1)S(1)} %get-tuple-element.30), channel_id=1, source_target_pairs={{0,224},{1,33},{32,0},{33,65},{64,32},{65,97},{96,64},{97,129},{12... | collective-permute-start | bytes 688136 | tf_op jit(solution)/shard_map/ppermute | solution.py:35
  93.3 10.2 %collective-permute-start.11 = (bf16[16,3584]{1,0:T(8,128)(2,1)S(1)}, bf16[16,3584]{1,0:T(8,128)(2,1)S(1)}, u32[]{:S(2)}, u32[]{:S(2)}) collective-permute-start(bf16[16,3584]{1,0:T(8,128)(2,1)S(1)} %get-tuple-element.31), channel_id=1, source_target_pairs={{0,192},{1,65},{32,224},{33,97},{64,0},{65,129},{96,32},{97,161},{... | collective-permute-start | bytes 344072 | tf_op jit(solution)/shard_map/ppermute | solution.py:35
  93.7 15.1 %collective-permute-start.8 = (bf16[16,3584]{1,0:T(8,128)(2,1)S(1)}, bf16[16,3584]{1,0:T(8,128)(2,1)S(1)}, u32[]{:S(2)}, u32[]{:S(2)}) collective-permute-start(bf16[16,3584]{1,0:T(8,128)(2,1)S(1)} %get-tuple-element.27), channel_id=1, source_target_pairs={{0,224},{1,33},{32,0},{33,65},{64,32},{65,97},{96,64},{97,129},{12... | collective-permute-start | bytes 344072 | tf_op jit(solution)/shard_map/ppermute | solution.py:35
  94.0 14.8 %collective-permute-start.9 = (bf16[16,3584]{1,0:T(8,128)(2,1)S(1)}, bf16[16,3584]{1,0:T(8,128)(2,1)S(1)}, u32[]{:S(2)}, u32[]{:S(2)}) collective-permute-start(bf16[16,3584]{1,0:T(8,128)(2,1)S(1)} %get-tuple-element.28), channel_id=1, source_target_pairs={{0,225},{1,32},{32,1},{33,64},{64,33},{65,96},{96,65},{97,128},{12... | collective-permute-start | bytes 344072 | tf_op jit(solution)/shard_map/ppermute | solution.py:39
  103.5 5.8 %collective-permute-start.12 = (bf16[16,3584]{1,0:T(8,128)(2,1)S(1)}, bf16[16,3584]{1,0:T(8,128)(2,1)S(1)}, u32[]{:S(2)}, u32[]{:S(2)}) collective-permute-start(bf16[16,3584]{1,0:T(8,128)(2,1)S(1)} %get-tuple-element.33), channel_id=1, source_target_pairs={{0,192},{1,65},{32,224},{33,97},{64,0},{65,129},{96,32},{97,161},{... | collective-permute-start | bytes 344072 | tf_op jit(solution)/shard_map/ppermute | solution.py:35
  104.6 9.5 %collective-permute-start.13 = (bf16[16,3584]{1,0:T(8,128)(2,1)S(1)}, bf16[16,3584]{1,0:T(8,128)(2,1)S(1)}, u32[]{:S(2)}, u32[]{:S(2)}) collective-permute-start(bf16[16,3584]{1,0:T(8,128)(2,1)S(1)} %get-tuple-element.34), channel_id=1, source_target_pairs={{0,193},{1,64},{32,225},{33,96},{64,1},{65,128},{96,33},{97,160},{... | collective-permute-start | bytes 344072 | tf_op jit(solution)/shard_map/ppermute | solution.py:39

commit v3 on v2

--- a/solution.py
+++ b/solution.py
@@ -5,8 +5,8 @@
 from jax.experimental.pallas import tpu as pltpu
 from jax.sharding import Mesh, PartitionSpec as P
 
-Z, Y, X, C = 8, 4, 4, 2
-PLANE = Y * X
+Z, PAIR, Y, X, C = 4, 2, 4, 4, 2
+PLANE = PAIR * Y * X
 SLOTS = 2
 TAIL = 128
 BF = jnp.bfloat16
@@ -32,11 +32,11 @@
 
 
 def send(value, shift):
-    return lax.ppermute(value, ("z", "c"), along(shift))
+    return lax.ppermute(value, ("s", "c"), along(shift))
 
 
 def back_across(value, shift):
-    return lax.ppermute(value, ("z", "c"), across(shift))
+    return lax.ppermute(value, ("s", "c"), across(shift))
 
 
 def swap(value):
@@ -83,7 +83,7 @@
     if rows < TAIL:
         tail.append(jnp.zeros((TAIL - rows, TAIL), F32))
     tail = jnp.concatenate(tail, axis=0).T[:, :rows]
-    expert = (lax.axis_index("z") * PLANE + lax.broadcasted_iota(jnp.int32, (PLANE, rows), 0)).astype(F32)
+    expert = (lax.axis_index("s") * PLANE + lax.broadcasted_iota(jnp.int32, (PLANE, rows), 0)).astype(F32)
     named = jnp.zeros((PLANE, rows), F32)
     gate = jnp.zeros((PLANE, rows), F32)
     for k in range(8):
@@ -208,7 +208,7 @@
 
 def exchange(value):
     width = value.shape[1]
-    return lax.all_to_all(value.reshape(PLANE, -1, width), ("y", "x"), 0, 0, tiled=True).reshape(-1, width)
+    return lax.all_to_all(value.reshape(PLANE, -1, width), ("p", "y", "x"), 0, 0, tiled=True).reshape(-1, width)
 
 
 def body(tokens, expert_ids, gates, gate_weight, up_weight, down_weight):
@@ -218,29 +218,25 @@
     other, sent_weights = lax.optimization_barrier((swap(own), own_weights))
     other_weights = [swap(w) for w in sent_weights]
     own_weights = [pltpu.with_memory_space_constraint(w, pltpu.HBM) for w in own_weights]
+
+    both = jnp.concatenate([own, other], axis=0)
+    far = send(own, 2)
+    near = send(both, 1)
+    rows, high, low = place((both, near, far), block, width)
+    rows, other_weights = lax.optimization_barrier((rows, other_weights))
     other_weights = [pltpu.with_memory_space_constraint(w, pltpu.VMEM) for w in other_weights]
-
-    both = jnp.concatenate([own, other], axis=0)
-    second = send(both, 2)
-    near = send(both, 1)
-    third = send(second, 1)
-    fourth = send(second[:block], 2)
-    rows, high, low = place((both, near, second, third, fourth), block, width)
     done = experts(exchange(rows), own_weights, other_weights)
     returned = exchange(done)
-    shapes = ((block, F32), (block, BF), (block, BF), (block, F32), (block, F32), (2 * block, BF), (block, BF))
-    q_own, q_near, q_near_other, q_second, q_second_other, q_third, q_fourth = collect(returned, high, low, shapes)
-    third = send(q_third, -1)
-    fourth = send(q_fourth, -2)
+    shapes = ((block, F32), (block, BF), (block, BF), (block, BF))
+    q_own, q_near, q_near_other, q_far = collect(returned, high, low, shapes)
+    far = send(q_far, -2)
     near = send(q_near, -1)
     near_other = back_across(q_near_other, 1)
-    second = send((q_second + third[:block].astype(F32) + fourth.astype(F32)).astype(BF), -2)
-    second_other = back_across((q_second_other + third[block:].astype(F32)).astype(BF), 2)
-    total = q_own + near.astype(F32) + near_other.astype(F32)
-    return (total + second.astype(F32) + second_other.astype(F32)).astype(BF)
+    return (q_own + near.astype(F32) + near_other.astype(F32) + far.astype(F32)).astype(BF)
 
 
 def solution(mesh):
-    fine = Mesh(mesh.devices.reshape(Z, Y, X, C), ("z", "y", "x", "c"))
-    rows = P(("z", "y", "x", "c"))
+    names = ("s", "p", "y", "x", "c")
+    fine = Mesh(mesh.devices.reshape(Z, PAIR, Y, X, C), names)
+    rows = P(names)
     return jax.shard_map(body, mesh=fine, in_specs=(rows,) * 6, out_specs=rows, check_vma=False)

time: 116 us -> 111 us (0.957)
  starting transfers between devices: 32 us -> 18.2 us
  blocking collectives: 55.5 us -> 60.7 us
  waiting for transfers between devices: 15 us -> 18.6 us
    ppermute x10 -> x5, starting transfers between devices: 27.9 us -> 14 us  [the longest x4 8.66 us: send(): return lax.ppermute(value, ('s', 'c'), along(shift))]
    all_to_all x2, blocking collectives: 55.5 us -> 60.7 us  [exchange(): lax.all_to_all(value.reshape(PLANE, -1, width), ('p', 'y', 'x'), 0, 0, ti...]
    ppermute x10 -> x5, waiting for transfers between devices: 13.8 us -> 17.4 us  [the longest x4 12.2 us: send(): return lax.ppermute(value, ('s', 'c'), along(shift))]
  transfers between devices with their start and end apart: 14 -> 9, of which waited for: 7 -> 4; matrix products, arithmetic and copies ran while one was open for 1% -> 1% of each run, Pallas kernels for 1% -> 1%
where the time goes in v3:
time: 111 us; the launch traced here: 110 us
  blocking collectives  60.7 us (55%)
  waiting for transfers between devices  18.6 us (17%)
  starting transfers between devices  18.2 us (16%)
  Pallas kernels  10.7 us (10%)
  other arithmetic  1.62 us (1%)
    all_to_all x2, blocking collectives, exchange(): lax.all_to_all(value.reshape(PLANE, -1, width), ('p', 'y', 'x'), 0, 0, ti...  60.7 us
    ppermute x4, waiting for transfers between devices, send(): return lax.ppermute(value, ('s', 'c'), along(shift))  12.2 us
    ppermute x4, starting transfers between devices, send(): return lax.ppermute(value, ('s', 'c'), along(shift))  8.66 us
    pallas_call x1, Pallas kernels, experts(): pl.pallas_call(expert_kernel, out_shape=jax.ShapeDtypeStruct(rows.shape,...  7.33 us
    ppermute x1, starting transfers between devices, back_across(): return lax.ppermute(value, ('s', 'c'), across(shift))  5.38 us
    ppermute x1, waiting for transfers between devices, back_across(): return lax.ppermute(value, ('s', 'c'), across(shift))  5.14 us
    ppermute x4, starting transfers between devices, swap(): return lax.ppermute(value, 'c', [(0, 1), (1, 0)])  4.11 us
  transfers between devices with their start and end apart: 9, of which 4 were waited for; matrix products, arithmetic and copies ran while one was open for 1% of the time, Pallas kernels for 1%

profile of v3, /device:TPU:1, one launch (start us, length us, event | category | flops | bytes accessed | tf_op | source)
XLA Modules:
  0.0 109.8 jit_solution(3747097471112010292)
XLA Ops:
  0.0 1.7 %extend.1 = bf16[16,3712]{1,0:T(8,128)(2,1)} custom-call(bf16[16,3584]{1,0:T(8,128)(2,1)} %tokens.1, s32[8,16]{1,0:T(8,128)} %bitcast.19, f32[8,16]{1,0:T(8,128)} %bitcast.20), custom_call_target="tpu_custom_call" | custom-call | tf_op jit(solution)/shard_map/extend/pallas_call | solution.py:67
  1.7 3.2 %collective-permute-start = (bf16[16,3712]{1,0:T(8,128)(2,1)}, bf16[16,3712]{1,0:T(8,128)(2,1)S(1)}, u32[]{:S(2)}, u32[]{:S(2)}) collective-permute-start(bf16[16,3712]{1,0:T(8,128)(2,1)} %extend.1), channel_id=1, source_target_pairs={{0,1},{1,0},{2,3},{3,2},{4,5},{5,4},{6,7},{7,6},{8,9},{9,8},{10,11... | collective-permute-start | bytes 356360 | tf_op jit(solution)/shard_map/ppermute | solution.py:43
  4.9 1.2 %collective-permute-done = bf16[16,3712]{1,0:T(8,128)(2,1)S(1)} collective-permute-done((bf16[16,3712]{1,0:T(8,128)(2,1)}, bf16[16,3712]{1,0:T(8,128)(2,1)S(1)}, u32[]{:S(2)}, u32[]{:S(2)}) %collective-permute-start) | collective-permute-done | bytes 118816 | tf_op jit(solution)/shard_map/ppermute | solution.py:43
  6.1 0.4 collective-permute-start.3
  6.5 0.2 collective-permute-start.4
  6.6 0.4 collective-permute-start.5
  7.0 0.9 pad_maximum_fusion.refs_0_
  7.9 4.4 %collective-permute-start.1 = (bf16[32,3712]{1,0:T(8,128)(2,1)S(1)}, bf16[32,3712]{1,0:T(8,128)(2,1)S(1)}, u32[]{:S(2)}, u32[]{:S(2)}) collective-permute-start(bf16[32,3712]{1,0:T(8,128)(2,1)S(1)} %pad_maximum_fusion.refs_0_), channel_id=1, source_target_pairs={{0,64},{1,193},{64,128},{65,1},{128,192},{129,65},{192,0},{193,129... | collective-permute-start | bytes 712712 | tf_op jit(solution)/shard_map/ppermute | solution.py:35
  12.3 1.0 collective-permute-start.2
  13.3 10.6 %collective-permute-done.2.refs_2_ = bf16[16,3712]{1,0:T(8,128)(2,1)S(1)} collective-permute-done((bf16[16,3712]{1,0:T(8,128)(2,1)}, bf16[16,3712]{1,0:T(8,128)(2,1)S(1)}, u32[]{:S(2)}, u32[]{:S(2)}) %collective-permute-start.2) | collective-permute-done | bytes 118816 | tf_op jit(solution)/shard_map/ppermute | solution.py:35
  23.8 0.0 collective-permute-done.1.refs_1_
  23.8 0.9 place.1
  24.7 0.0 collective-permute-done.3.gate_b
  24.7 0.0 collective-permute-done.4.up_b
  24.7 0.0 collective-permute-done.5.down_b
  24.7 31.8 %all_to_all.10 = bf16[32,8,3584]{2,1,0:T(8,128)(2,1)S(1)} all-to-all(bf16[32,8,3584]{2,1,0:T(8,128)(2,1)S(1)} %bitcast.12), channel_id=1, replica_groups=mesh['s'=4,'p'=2,'y'=4,'x'=4,'c'=2] {'p','y','x'}, dimensions={0} | all-to-all | bytes 3670016 | tf_op jit(solution)/shard_map/all_to_all | solution.py:211
  56.5 7.3 %experts.1 = bf16[256,3584]{1,0:T(8,128)(2,1)S(1)} custom-call(bf16[256,3584]{1,0:T(8,128)(2,1)S(1)} %bitcast.9, bf16[3584,512]{1,0:T(8,128)(2,1)} %bitcast.14, bf16[3584,512]{1,0:T(8,128)(2,1)} %bitcast.16, bf16[512,3584]{1,0:T(8,128)(2,1)} %bitcast.18, bf16[3584,512]{1,0:T(8,128)(2,1)S(1)} %collective-permute-done.3.gate_b, ...), custom_call_target="tpu_custom_call" | custom-call | flops 5637144576 | bytes 25690112 | tf_op jit(solution)/shard_map/experts/pallas_call | solution.py:163
  63.9 28.9 %all_to_all.11 = bf16[32,8,3584]{2,1,0:T(8,128)(2,1)S(1)} all-to-all(bf16[32,8,3584]{2,1,0:T(8,128)(2,1)S(1)} %bitcast.10), channel_id=1, replica_groups=mesh['s'=4,'p'=2,'y'=4,'x'=4,'c'=2] {'p','y','x'}, dimensions={0} | all-to-all | bytes 3670016 | tf_op jit(solution)/shard_map/all_to_all | solution.py:211
  92.8 0.8 collect.1
  93.5 0.2 collective-permute-start.6
  93.7 5.4 %collective-permute-start.7 = (bf16[16,3584]{1,0:T(8,128)(2,1)S(1)}, bf16[16,3584]{1,0:T(8,128)(2,1)S(1)}, u32[]{:S(2)}, u32[]{:S(2)}) collective-permute-start(bf16[16,3584]{1,0:T(8,128)(2,1)S(1)} %get-tuple-element.33), channel_id=1, source_target_pairs={{0,193},{1,64},{64,1},{65,128},{128,65},{129,192},{192,129},{193,0... | collective-permute-start | bytes 344072 | tf_op jit(solution)/shard_map/ppermute | solution.py:39
  99.1 3.1 %collective-permute-start.8 = (bf16[16,3584]{1,0:T(8,128)(2,1)S(1)}, bf16[16,3584]{1,0:T(8,128)(2,1)S(1)}, u32[]{:S(2)}, u32[]{:S(2)}) collective-permute-start(bf16[16,3584]{1,0:T(8,128)(2,1)S(1)} %get-tuple-element.34), channel_id=1, source_target_pairs={{0,128},{1,129},{64,192},{65,193},{128,0},{129,1},{192,64},{193,65... | collective-permute-start | bytes 344072 | tf_op jit(solution)/shard_map/ppermute | solution.py:35
  102.2 0.0 collective-permute-done.6
  102.2 5.1 %collective-permute-done.7 = bf16[16,3584]{1,0:T(8,128)(2,1)S(1)} collective-permute-done((bf16[16,3584]{1,0:T(8,128)(2,1)S(1)}, bf16[16,3584]{1,0:T(8,128)(2,1)S(1)}, u32[]{:S(2)}, u32[]{:S(2)}) %collective-permute-start.7) | collective-permute-done | bytes 114720 | tf_op jit(solution)/shard_map/ppermute | solution.py:39
  107.4 1.7 %collective-permute-done.8 = bf16[16,3584]{1,0:T(8,128)(2,1)S(1)} collective-permute-done((bf16[16,3584]{1,0:T(8,128)(2,1)S(1)}, bf16[16,3584]{1,0:T(8,128)(2,1)S(1)}, u32[]{:S(2)}, u32[]{:S(2)}) %collective-permute-start.8) | collective-permute-done | bytes 114720 | tf_op jit(solution)/shard_map/ppermute | solution.py:35
  109.1 0.7 add_convert_fusion
Async XLA Ops:
  1.7 4.4 %collective-permute-start = (bf16[16,3712]{1,0:T(8,128)(2,1)}, bf16[16,3712]{1,0:T(8,128)(2,1)S(1)}, u32[]{:S(2)}, u32[]{:S(2)}) collective-permute-start(bf16[16,3712]{1,0:T(8,128)(2,1)} %extend.1), channel_id=1, source_target_pairs={{0,1},{1,0},{2,3},{3,2},{4,5},{5,4},{6,7},{7,6},{8,9},{9,8},{10,11... | collective-permute-start | bytes 356360 | tf_op jit(solution)/shard_map/ppermute | solution.py:43
  6.1 18.6 %collective-permute-start.3 = (bf16[3584,512]{1,0:T(8,128)(2,1)}, bf16[3584,512]{1,0:T(8,128)(2,1)S(1)}, u32[]{:S(2)}, u32[]{:S(2)}) collective-permute-start(bf16[3584,512]{1,0:T(8,128)(2,1)} %bitcast.13), channel_id=1, source_target_pairs={{0,1},{1,0},{2,3},{3,2},{4,5},{5,4},{6,7},{7,6},{8,9},{9,8},{10,11... | collective-permute-start | bytes 11010056 | tf_op jit(solution)/shard_map/ppermute | solution.py:43
  6.5 18.3 %collective-permute-start.4 = (bf16[3584,512]{1,0:T(8,128)(2,1)}, bf16[3584,512]{1,0:T(8,128)(2,1)S(1)}, u32[]{:S(2)}, u32[]{:S(2)}) collective-permute-start(bf16[3584,512]{1,0:T(8,128)(2,1)} %bitcast.15), channel_id=1, source_target_pairs={{0,1},{1,0},{2,3},{3,2},{4,5},{5,4},{6,7},{7,6},{8,9},{9,8},{10,11... | collective-permute-start | bytes 11010056 | tf_op jit(solution)/shard_map/ppermute | solution.py:43
  6.6 18.1 %collective-permute-start.5 = (bf16[512,3584]{1,0:T(8,128)(2,1)}, bf16[512,3584]{1,0:T(8,128)(2,1)S(1)}, u32[]{:S(2)}, u32[]{:S(2)}) collective-permute-start(bf16[512,3584]{1,0:T(8,128)(2,1)} %bitcast.17), channel_id=1, source_target_pairs={{0,1},{1,0},{2,3},{3,2},{4,5},{5,4},{6,7},{7,6},{8,9},{9,8},{10,11... | collective-permute-start | bytes 11010056 | tf_op jit(solution)/shard_map/ppermute | solution.py:43
  7.9 15.9 %collective-permute-start.1 = (bf16[32,3712]{1,0:T(8,128)(2,1)S(1)}, bf16[32,3712]{1,0:T(8,128)(2,1)S(1)}, u32[]{:S(2)}, u32[]{:S(2)}) collective-permute-start(bf16[32,3712]{1,0:T(8,128)(2,1)S(1)} %pad_maximum_fusion.refs_0_), channel_id=1, source_target_pairs={{0,64},{1,193},{64,128},{65,1},{128,192},{129,65},{192,0},{193,129... | collective-permute-start | bytes 712712 | tf_op jit(solution)/shard_map/ppermute | solution.py:35
  12.3 11.6 %collective-permute-start.2 = (bf16[16,3712]{1,0:T(8,128)(2,1)}, bf16[16,3712]{1,0:T(8,128)(2,1)S(1)}, u32[]{:S(2)}, u32[]{:S(2)}) collective-permute-start(bf16[16,3712]{1,0:T(8,128)(2,1)} %extend.1), channel_id=1, source_target_pairs={{0,128},{1,129},{64,192},{65,193},{128,0},{129,1},{192,64},{193,65... | collective-permute-start | bytes 356360 | tf_op jit(solution)/shard_map/ppermute | solution.py:35
  93.5 8.7 %collective-permute-start.6 = (bf16[16,3584]{1,0:T(8,128)(2,1)S(1)}, bf16[16,3584]{1,0:T(8,128)(2,1)S(1)}, u32[]{:S(2)}, u32[]{:S(2)}) collective-permute-start(bf16[16,3584]{1,0:T(8,128)(2,1)S(1)} %get-tuple-element.32), channel_id=1, source_target_pairs={{0,192},{1,65},{64,0},{65,129},{128,64},{129,193},{192,128},{193,1... | collective-permute-start | bytes 344072 | tf_op jit(solution)/shard_map/ppermute | solution.py:35
  93.7 13.7 %collective-permute-start.7 = (bf16[16,3584]{1,0:T(8,128)(2,1)S(1)}, bf16[16,3584]{1,0:T(8,128)(2,1)S(1)}, u32[]{:S(2)}, u32[]{:S(2)}) collective-permute-start(bf16[16,3584]{1,0:T(8,128)(2,1)S(1)} %get-tuple-element.33), channel_id=1, source_target_pairs={{0,193},{1,64},{64,1},{65,128},{128,65},{129,192},{192,129},{193,0... | collective-permute-start | bytes 344072 | tf_op jit(solution)/shard_map/ppermute | solution.py:39
  99.1 9.9 %collective-permute-start.8 = (bf16[16,3584]{1,0:T(8,128)(2,1)S(1)}, bf16[16,3584]{1,0:T(8,128)(2,1)S(1)}, u32[]{:S(2)}, u32[]{:S(2)}) collective-permute-start(bf16[16,3584]{1,0:T(8,128)(2,1)S(1)} %get-tuple-element.34), channel_id=1, source_target_pairs={{0,128},{1,129},{64,192},{65,193},{128,0},{129,1},{192,64},{193,65... | collective-permute-start | bytes 344072 | tf_op jit(solution)/shard_map/ppermute | solution.py:35

commit v4 on v3

--- a/solution.py
+++ b/solution.py
@@ -67,8 +67,9 @@
     return pl.pallas_call(
         extend_kernel,
         out_shape=jax.ShapeDtypeStruct((block, width + TAIL), BF),
+        compiler_params=pltpu.CompilerParams(vmem_limit_bytes=4 * MIB),
         name="extend",
-    )(tokens, expert_ids.T, gates.T)
+    )(*[pltpu.with_memory_space_constraint(v, pltpu.HBM) for v in (tokens, expert_ids.T, gates.T)])
 
 
 def place_kernel(block, *refs):
@@ -83,7 +84,9 @@
     if rows < TAIL:
         tail.append(jnp.zeros((TAIL - rows, TAIL), F32))
     tail = jnp.concatenate(tail, axis=0).T[:, :rows]
-    expert = (lax.axis_index("s") * PLANE + lax.broadcasted_iota(jnp.int32, (PLANE, rows), 0)).astype(F32)
+    peer = lax.broadcasted_iota(jnp.int32, (PLANE, rows), 0)
+    peer = (peer // Y % PAIR * Y + peer % Y) * X + peer // (Y * PAIR)
+    expert = (lax.axis_index("s") * PLANE + peer).astype(F32)
     named = jnp.zeros((PLANE, rows), F32)
     gate = jnp.zeros((PLANE, rows), F32)
     for k in range(8):
@@ -208,15 +211,15 @@
 
 def exchange(value):
     width = value.shape[1]
-    return lax.all_to_all(value.reshape(PLANE, -1, width), ("p", "y", "x"), 0, 0, tiled=True).reshape(-1, width)
+    return lax.all_to_all(value.reshape(PLANE, -1, width), ("x", "p", "y"), 0, 0, tiled=True).reshape(-1, width)
 
 
 def body(tokens, expert_ids, gates, gate_weight, up_weight, down_weight):
     block, width = tokens.shape
     own_weights = [gate_weight[0], up_weight[0], down_weight[0]]
     own = extend(tokens, expert_ids, gates)
-    other, sent_weights = lax.optimization_barrier((swap(own), own_weights))
-    other_weights = [swap(w) for w in sent_weights]
+    other, sent_weights = lax.optimization_barrier((swap(own), own_weights[1:]))
+    other_weights = [swap(w) for w in own_weights[:1] + sent_weights]
     own_weights = [pltpu.with_memory_space_constraint(w, pltpu.HBM) for w in own_weights]
 
     both = jnp.concatenate([own, other], axis=0)

time: 111 us -> 108 us (0.973)
    ppermute x4, waiting for transfers between devices: 12.2 us -> 14.2 us  [send(): return lax.ppermute(value, ('s', 'c'), along(shift))]
    ppermute x1, waiting for transfers between devices: 5.14 us -> 3.38 us  [back_across(): return lax.ppermute(value, ('s', 'c'), across(shift))]
  transfers between devices with their start and end apart: 9 -> 9, of which waited for: 4 -> 4; matrix products, arithmetic and copies ran while one was open for 1% -> 0% of each run, Pallas kernels for 1% -> 1%
where the time goes in v4:
time: 108 us
  blocking collectives  60.1 us (56%)
  starting transfers between devices  18.4 us (17%)
  waiting for transfers between devices  18.4 us (17%)
  Pallas kernels  10 us (9%)
    all_to_all x2, blocking collectives, exchange(): lax.all_to_all(value.reshape(PLANE, -1, width), ('x', 'p', 'y'), 0, 0, ti...  60.1 us
    ppermute x4, waiting for transfers between devices, send(): return lax.ppermute(value, ('s', 'c'), along(shift))  14.2 us
    ppermute x4, starting transfers between devices, send(): return lax.ppermute(value, ('s', 'c'), along(shift))  8.81 us
    pallas_call x1, Pallas kernels, experts(): pl.pallas_call(expert_kernel, out_shape=jax.ShapeDtypeStruct(rows.shape,...  7.33 us
    ppermute x1, starting transfers between devices, back_across(): return lax.ppermute(value, ('s', 'c'), across(shift))  5.77 us
    ppermute x4, starting transfers between devices, swap(): return lax.ppermute(value, 'c', [(0, 1), (1, 0)])  3.83 us
    ppermute x1, waiting for transfers between devices, back_across(): return lax.ppermute(value, ('s', 'c'), across(shift))  3.38 us
  transfers between devices with their start and end apart: 9, of which 4 were waited for; matrix products, arithmetic and copies ran while one was open for 0% of the time, Pallas kernels for 1%

profile of v4, /device:TPU:1, one launch (start us, length us, event | category | flops | bytes accessed | tf_op | source)
XLA Modules:
  0.0 107.7 jit_solution(12758823663969629192)
XLA Ops:
  0.0 1.0 extend.1
  1.0 3.2 %collective-permute-start = (bf16[16,3712]{1,0:T(8,128)(2,1)S(1)}, bf16[16,3712]{1,0:T(8,128)(2,1)S(1)}, u32[]{:S(2)}, u32[]{:S(2)}) collective-permute-start(bf16[16,3712]{1,0:T(8,128)(2,1)S(1)} %extend.1), channel_id=1, source_target_pairs={{0,1},{1,0},{2,3},{3,2},{4,5},{5,4},{6,7},{7,6},{8,9},{9,8},{10,11... | collective-permute-start | bytes 356360 | tf_op jit(solution)/shard_map/ppermute | solution.py:43
  4.3 0.1 collective-permute-start.3
  4.4 0.9 collective-permute-done
  5.3 0.4 collective-permute-start.4
  5.6 0.2 collective-permute-start.5
  5.8 4.4 %collective-permute-start.1 = (bf16[32,3712]{1,0:T(8,128)(2,1)S(1)}, bf16[32,3712]{1,0:T(8,128)(2,1)S(1)}, u32[]{:S(2)}, u32[]{:S(2)}) collective-permute-start(bf16[32,3712]{1,0:T(8,128)(2,1)S(1)} %pad_maximum_fusion.refs_0_), channel_id=1, source_target_pairs={{0,64},{1,193},{64,128},{65,1},{128,192},{129,65},{192,0},{193,129... | collective-permute-start | bytes 712712 | tf_op jit(solution)/shard_map/ppermute | solution.py:35
  10.2 1.0 collective-permute-start.2
  11.1 9.8 %collective-permute-done.2.refs_2_ = bf16[16,3712]{1,0:T(8,128)(2,1)S(1)} collective-permute-done((bf16[16,3712]{1,0:T(8,128)(2,1)S(1)}, bf16[16,3712]{1,0:T(8,128)(2,1)S(1)}, u32[]{:S(2)}, u32[]{:S(2)}) %collective-permute-start.2) | collective-permute-done | bytes 118816 | tf_op jit(solution)/shard_map/ppermute | solution.py:35
  21.0 0.0 collective-permute-done.1.refs_1_
  21.0 0.9 place.1
  21.9 0.0 collective-permute-done.3.gate_b
  21.9 0.0 collective-permute-done.4.up_b
  21.9 0.0 collective-permute-done.5.down_b
  21.9 32.9 %all_to_all.10 = bf16[32,8,3584]{2,1,0:T(8,128)(2,1)S(1)} all-to-all(bf16[32,8,3584]{2,1,0:T(8,128)(2,1)S(1)} %bitcast.12), channel_id=1, replica_groups=mesh['s'=4,'p'=2,'y'=4,'x'=4,'c'=2] {'x','p','y'}, dimensions={0} | all-to-all | bytes 3670016 | tf_op jit(solution)/shard_map/all_to_all | solution.py:214
  54.8 7.3 %experts.1 = bf16[256,3584]{1,0:T(8,128)(2,1)S(1)} custom-call(bf16[256,3584]{1,0:T(8,128)(2,1)S(1)} %bitcast.9, bf16[3584,512]{1,0:T(8,128)(2,1)} %bitcast.14, bf16[3584,512]{1,0:T(8,128)(2,1)} %bitcast.16, bf16[512,3584]{1,0:T(8,128)(2,1)} %bitcast.18, bf16[3584,512]{1,0:T(8,128)(2,1)S(1)} %collective-permute-done.3.gate_b, ...), custom_call_target="tpu_custom_call" | custom-call | flops 5637144576 | bytes 25690112 | tf_op jit(solution)/shard_map/experts/pallas_call | solution.py:166
  62.2 27.1 %all_to_all.11 = bf16[32,8,3584]{2,1,0:T(8,128)(2,1)S(1)} all-to-all(bf16[32,8,3584]{2,1,0:T(8,128)(2,1)S(1)} %bitcast.10), channel_id=1, replica_groups=mesh['s'=4,'p'=2,'y'=4,'x'=4,'c'=2] {'x','p','y'}, dimensions={0} | all-to-all | bytes 3670016 | tf_op jit(solution)/shard_map/all_to_all | solution.py:214
  89.3 0.8 collect.1
  90.1 0.1 collective-permute-start.6
  90.1 5.8 %collective-permute-start.7 = (bf16[16,3584]{1,0:T(8,128)(2,1)S(1)}, bf16[16,3584]{1,0:T(8,128)(2,1)S(1)}, u32[]{:S(2)}, u32[]{:S(2)}) collective-permute-start(bf16[16,3584]{1,0:T(8,128)(2,1)S(1)} %get-tuple-element.31), channel_id=1, source_target_pairs={{0,193},{1,64},{64,1},{65,128},{128,65},{129,192},{192,129},{193,0... | collective-permute-start | bytes 344072 | tf_op jit(solution)/shard_map/ppermute | solution.py:39
  95.9 3.4 %collective-permute-start.8 = (bf16[16,3584]{1,0:T(8,128)(2,1)S(1)}, bf16[16,3584]{1,0:T(8,128)(2,1)S(1)}, u32[]{:S(2)}, u32[]{:S(2)}) collective-permute-start(bf16[16,3584]{1,0:T(8,128)(2,1)S(1)} %get-tuple-element.32), channel_id=1, source_target_pairs={{0,128},{1,129},{64,192},{65,193},{128,0},{129,1},{192,64},{193,65... | collective-permute-start | bytes 344072 | tf_op jit(solution)/shard_map/ppermute | solution.py:35
  99.3 0.0 collective-permute-done.6
  99.3 3.4 %collective-permute-done.7 = bf16[16,3584]{1,0:T(8,128)(2,1)S(1)} collective-permute-done((bf16[16,3584]{1,0:T(8,128)(2,1)S(1)}, bf16[16,3584]{1,0:T(8,128)(2,1)S(1)}, u32[]{:S(2)}, u32[]{:S(2)}) %collective-permute-start.7) | collective-permute-done | bytes 114720 | tf_op jit(solution)/shard_map/ppermute | solution.py:39
  102.7 4.3 %collective-permute-done.8 = bf16[16,3584]{1,0:T(8,128)(2,1)S(1)} collective-permute-done((bf16[16,3584]{1,0:T(8,128)(2,1)S(1)}, bf16[16,3584]{1,0:T(8,128)(2,1)S(1)}, u32[]{:S(2)}, u32[]{:S(2)}) %collective-permute-start.8) | collective-permute-done | bytes 114720 | tf_op jit(solution)/shard_map/ppermute | solution.py:35
  107.0 0.7 add_convert_fusion
  (1 shorter events, 0.0 us)
Async XLA Ops:
  1.0 4.2 %collective-permute-start = (bf16[16,3712]{1,0:T(8,128)(2,1)S(1)}, bf16[16,3712]{1,0:T(8,128)(2,1)S(1)}, u32[]{:S(2)}, u32[]{:S(2)}) collective-permute-start(bf16[16,3712]{1,0:T(8,128)(2,1)S(1)} %extend.1), channel_id=1, source_target_pairs={{0,1},{1,0},{2,3},{3,2},{4,5},{5,4},{6,7},{7,6},{8,9},{9,8},{10,11... | collective-permute-start | bytes 356360 | tf_op jit(solution)/shard_map/ppermute | solution.py:43
  4.3 17.6 %collective-permute-start.3 = (bf16[3584,512]{1,0:T(8,128)(2,1)}, bf16[3584,512]{1,0:T(8,128)(2,1)S(1)}, u32[]{:S(2)}, u32[]{:S(2)}) collective-permute-start(bf16[3584,512]{1,0:T(8,128)(2,1)} %bitcast.13), channel_id=1, source_target_pairs={{0,1},{1,0},{2,3},{3,2},{4,5},{5,4},{6,7},{7,6},{8,9},{9,8},{10,11... | collective-permute-start | bytes 11010056 | tf_op jit(solution)/shard_map/ppermute | solution.py:43
  5.3 16.6 %collective-permute-start.4 = (bf16[3584,512]{1,0:T(8,128)(2,1)}, bf16[3584,512]{1,0:T(8,128)(2,1)S(1)}, u32[]{:S(2)}, u32[]{:S(2)}) collective-permute-start(bf16[3584,512]{1,0:T(8,128)(2,1)} %bitcast.15), channel_id=1, source_target_pairs={{0,1},{1,0},{2,3},{3,2},{4,5},{5,4},{6,7},{7,6},{8,9},{9,8},{10,11... | collective-permute-start | bytes 11010056 | tf_op jit(solution)/shard_map/ppermute | solution.py:43
  5.6 16.3 %collective-permute-start.5 = (bf16[512,3584]{1,0:T(8,128)(2,1)}, bf16[512,3584]{1,0:T(8,128)(2,1)S(1)}, u32[]{:S(2)}, u32[]{:S(2)}) collective-permute-start(bf16[512,3584]{1,0:T(8,128)(2,1)} %bitcast.17), channel_id=1, source_target_pairs={{0,1},{1,0},{2,3},{3,2},{4,5},{5,4},{6,7},{7,6},{8,9},{9,8},{10,11... | collective-permute-start | bytes 11010056 | tf_op jit(solution)/shard_map/ppermute | solution.py:43
  5.8 15.2 %collective-permute-start.1 = (bf16[32,3712]{1,0:T(8,128)(2,1)S(1)}, bf16[32,3712]{1,0:T(8,128)(2,1)S(1)}, u32[]{:S(2)}, u32[]{:S(2)}) collective-permute-start(bf16[32,3712]{1,0:T(8,128)(2,1)S(1)} %pad_maximum_fusion.refs_0_), channel_id=1, source_target_pairs={{0,64},{1,193},{64,128},{65,1},{128,192},{129,65},{192,0},{193,129... | collective-permute-start | bytes 712712 | tf_op jit(solution)/shard_map/ppermute | solution.py:35
  10.2 10.8 %collective-permute-start.2 = (bf16[16,3712]{1,0:T(8,128)(2,1)S(1)}, bf16[16,3712]{1,0:T(8,128)(2,1)S(1)}, u32[]{:S(2)}, u32[]{:S(2)}) collective-permute-start(bf16[16,3712]{1,0:T(8,128)(2,1)S(1)} %extend.1), channel_id=1, source_target_pairs={{0,128},{1,129},{64,192},{65,193},{128,0},{129,1},{192,64},{193,65... | collective-permute-start | bytes 356360 | tf_op jit(solution)/shard_map/ppermute | solution.py:35
  90.1 9.2 %collective-permute-start.6 = (bf16[16,3584]{1,0:T(8,128)(2,1)S(1)}, bf16[16,3584]{1,0:T(8,128)(2,1)S(1)}, u32[]{:S(2)}, u32[]{:S(2)}) collective-permute-start(bf16[16,3584]{1,0:T(8,128)(2,1)S(1)} %get-tuple-element.30), channel_id=1, source_target_pairs={{0,192},{1,65},{64,0},{65,129},{128,64},{129,193},{192,128},{193,1... | collective-permute-start | bytes 344072 | tf_op jit(solution)/shard_map/ppermute | solution.py:35
  90.1 12.5 %collective-permute-start.7 = (bf16[16,3584]{1,0:T(8,128)(2,1)S(1)}, bf16[16,3584]{1,0:T(8,128)(2,1)S(1)}, u32[]{:S(2)}, u32[]{:S(2)}) collective-permute-start(bf16[16,3584]{1,0:T(8,128)(2,1)S(1)} %get-tuple-element.31), channel_id=1, source_target_pairs={{0,193},{1,64},{64,1},{65,128},{128,65},{129,192},{192,129},{193,0... | collective-permute-start | bytes 344072 | tf_op jit(solution)/shard_map/ppermute | solution.py:39
  95.9 11.1 %collective-permute-start.8 = (bf16[16,3584]{1,0:T(8,128)(2,1)S(1)}, bf16[16,3584]{1,0:T(8,128)(2,1)S(1)}, u32[]{:S(2)}, u32[]{:S(2)}) collective-permute-start(bf16[16,3584]{1,0:T(8,128)(2,1)S(1)} %get-tuple-element.32), channel_id=1, source_target_pairs={{0,128},{1,129},{64,192},{65,193},{128,0},{129,1},{192,64},{193,65... | collective-permute-start | bytes 344072 | tf_op jit(solution)/shard_map/ppermute | solution.py:35

commit v5 on v4

--- a/solution.py
+++ b/solution.py
@@ -85,6 +85,7 @@
         tail.append(jnp.zeros((TAIL - rows, TAIL), F32))
     tail = jnp.concatenate(tail, axis=0).T[:, :rows]
     peer = lax.broadcasted_iota(jnp.int32, (PLANE, rows), 0)
+    peer = peer + lax.axis_index("c") * (PLANE - 1 - 2 * peer)
     peer = (peer // Y % PAIR * Y + peer % Y) * X + peer // (Y * PAIR)
     expert = (lax.axis_index("s") * PLANE + peer).astype(F32)
     named = jnp.zeros((PLANE, rows), F32)
@@ -209,9 +210,22 @@
     )(returned, high, low)
 
 
+def groups():
+    out = []
+    for s in range(Z):
+        for c in range(C):
+            chips = [(p, y, x) for x in range(X) for p in range(PAIR) for y in range(Y)]
+            if c == 1:
+                chips = chips[::-1]
+            out.append([(((s * PAIR + p) * Y + y) * X + x) * C + c for p, y, x in chips])
+    return out
+
+
 def exchange(value):
     width = value.shape[1]
-    return lax.all_to_all(value.reshape(PLANE, -1, width), ("x", "p", "y"), 0, 0, tiled=True).reshape(-1, width)
+    blocks = value.reshape(PLANE, -1, width)
+    names = ("s", "p", "y", "x", "c")
+    return lax.all_to_all(blocks, names, 0, 0, axis_index_groups=groups(), tiled=True).reshape(-1, width)
 
 
 def body(tokens, expert_ids, gates, gate_weight, up_weight, down_weight):

time: 108 us -> 107 us (level); the launches traced: 108 us -> 105 us
  waiting for transfers between devices: 18.4 us -> 17.2 us
    ppermute x1, starting transfers between devices: 5.77 us -> 3.97 us  [back_across(): return lax.ppermute(value, ('s', 'c'), across(shift))]
    ppermute x1, waiting for transfers between devices: 3.38 us -> 1.87 us  [back_across(): return lax.ppermute(value, ('s', 'c'), across(shift))]
where the time goes in v5:
time: 107 us; the launch traced here: 105 us
  blocking collectives  59.9 us (56%)
  starting transfers between devices  17.5 us (16%)
  waiting for transfers between devices  17.2 us (16%)
  Pallas kernels  10 us (9%)
    all_to_all x2, blocking collectives, exchange(): lax.all_to_all(blocks, names, 0, 0, axis_index_groups=groups(), tiled=True)  59.9 us
    ppermute x4, waiting for transfers between devices, send(): return lax.ppermute(value, ('s', 'c'), along(shift))  14.4 us
    ppermute x4, starting transfers between devices, send(): return lax.ppermute(value, ('s', 'c'), along(shift))  9.75 us
    pallas_call x1, Pallas kernels, experts(): pl.pallas_call(expert_kernel, out_shape=jax.ShapeDtypeStruct(rows.shape,...  7.33 us
    ppermute x1, starting transfers between devices, back_across(): return lax.ppermute(value, ('s', 'c'), across(shift))  3.97 us
    ppermute x4, starting transfers between devices, swap(): return lax.ppermute(value, 'c', [(0, 1), (1, 0)])  3.83 us
  transfers between devices with their start and end apart: 9, of which 4 were waited for; matrix products, arithmetic and copies ran while one was open for 0% of the time, Pallas kernels for 1%

profile of v5, /device:TPU:1, one launch (start us, length us, event | category | flops | bytes accessed | tf_op | source)
XLA Modules:
  0.0 105.4 jit_solution(1587135845833667162)
XLA Ops:
  0.0 1.0 extend.1
  1.0 3.2 %collective-permute-start = (bf16[16,3712]{1,0:T(8,128)(2,1)S(1)}, bf16[16,3712]{1,0:T(8,128)(2,1)S(1)}, u32[]{:S(2)}, u32[]{:S(2)}) collective-permute-start(bf16[16,3712]{1,0:T(8,128)(2,1)S(1)} %extend.1), channel_id=1, source_target_pairs={{0,1},{1,0},{2,3},{3,2},{4,5},{5,4},{6,7},{7,6},{8,9},{9,8},{10,11... | collective-permute-start | bytes 356360 | tf_op jit(solution)/shard_map/ppermute | solution.py:43
  4.3 0.1 collective-permute-start.3
  4.4 0.9 collective-permute-done
  5.3 0.4 collective-permute-start.4
  5.6 0.2 collective-permute-start.5
  5.8 4.4 %collective-permute-start.1 = (bf16[32,3712]{1,0:T(8,128)(2,1)S(1)}, bf16[32,3712]{1,0:T(8,128)(2,1)S(1)}, u32[]{:S(2)}, u32[]{:S(2)}) collective-permute-start(bf16[32,3712]{1,0:T(8,128)(2,1)S(1)} %pad_maximum_fusion.refs_0_), channel_id=1, source_target_pairs={{0,64},{1,193},{64,128},{65,1},{128,192},{129,65},{192,0},{193,129... | collective-permute-start | bytes 712712 | tf_op jit(solution)/shard_map/ppermute | solution.py:35
  10.2 1.0 collective-permute-start.2
  11.1 9.8 %collective-permute-done.2.refs_2_ = bf16[16,3712]{1,0:T(8,128)(2,1)S(1)} collective-permute-done((bf16[16,3712]{1,0:T(8,128)(2,1)S(1)}, bf16[16,3712]{1,0:T(8,128)(2,1)S(1)}, u32[]{:S(2)}, u32[]{:S(2)}) %collective-permute-start.2) | collective-permute-done | bytes 118816 | tf_op jit(solution)/shard_map/ppermute | solution.py:35
  21.0 0.0 collective-permute-done.1.refs_1_
  21.0 0.9 place.1
  21.9 0.0 collective-permute-done.3.gate_b
  21.9 0.0 collective-permute-done.4.up_b
  21.9 0.0 collective-permute-done.5.down_b
  21.9 30.6 %all_to_all.10 = bf16[32,8,3584]{2,1,0:T(8,128)(2,1)S(1)} all-to-all(bf16[32,8,3584]{2,1,0:T(8,128)(2,1)S(1)} %bitcast.12), channel_id=1, replica_groups={{0,8,16,24,32,40,48,56,2,10,18,26,34,42,50,58,4,12,20,28,36,44,52,60,6,..., dimensions={0} | all-to-all | bytes 3670016 | tf_op jit(solution)/shard_map/all_to_all | solution.py:228
  52.5 7.3 %experts.1 = bf16[256,3584]{1,0:T(8,128)(2,1)S(1)} custom-call(bf16[256,3584]{1,0:T(8,128)(2,1)S(1)} %bitcast.9, bf16[3584,512]{1,0:T(8,128)(2,1)} %bitcast.14, bf16[3584,512]{1,0:T(8,128)(2,1)} %bitcast.16, bf16[512,3584]{1,0:T(8,128)(2,1)} %bitcast.18, bf16[3584,512]{1,0:T(8,128)(2,1)S(1)} %collective-permute-done.3.gate_b, ...), custom_call_target="tpu_custom_call" | custom-call | flops 5637144576 | bytes 25690112 | tf_op jit(solution)/shard_map/experts/pallas_call | solution.py:167
  59.8 29.3 %all_to_all.11 = bf16[32,8,3584]{2,1,0:T(8,128)(2,1)S(1)} all-to-all(bf16[32,8,3584]{2,1,0:T(8,128)(2,1)S(1)} %bitcast.10), channel_id=1, replica_groups={{0,8,16,24,32,40,48,56,2,10,18,26,34,42,50,58,4,12,20,28,36,44,52,60,6,..., dimensions={0} | all-to-all | bytes 3670016 | tf_op jit(solution)/shard_map/all_to_all | solution.py:228
  89.1 0.8 collect.1
  89.9 0.1 collective-permute-start.6
  90.0 4.0 %collective-permute-start.7 = (bf16[16,3584]{1,0:T(8,128)(2,1)S(1)}, bf16[16,3584]{1,0:T(8,128)(2,1)S(1)}, u32[]{:S(2)}, u32[]{:S(2)}) collective-permute-start(bf16[16,3584]{1,0:T(8,128)(2,1)S(1)} %get-tuple-element.31), channel_id=1, source_target_pairs={{0,193},{1,64},{64,1},{65,128},{128,65},{129,192},{192,129},{193,0... | collective-permute-start | bytes 344072 | tf_op jit(solution)/shard_map/ppermute | solution.py:39
  94.0 4.3 %collective-permute-start.8 = (bf16[16,3584]{1,0:T(8,128)(2,1)S(1)}, bf16[16,3584]{1,0:T(8,128)(2,1)S(1)}, u32[]{:S(2)}, u32[]{:S(2)}) collective-permute-start(bf16[16,3584]{1,0:T(8,128)(2,1)S(1)} %get-tuple-element.32), channel_id=1, source_target_pairs={{0,128},{1,129},{64,192},{65,193},{128,0},{129,1},{192,64},{193,65... | collective-permute-start | bytes 344072 | tf_op jit(solution)/shard_map/ppermute | solution.py:35
  98.3 0.0 collective-permute-done.6
  98.3 1.9 %collective-permute-done.7 = bf16[16,3584]{1,0:T(8,128)(2,1)S(1)} collective-permute-done((bf16[16,3584]{1,0:T(8,128)(2,1)S(1)}, bf16[16,3584]{1,0:T(8,128)(2,1)S(1)}, u32[]{:S(2)}, u32[]{:S(2)}) %collective-permute-start.7) | collective-permute-done | bytes 114720 | tf_op jit(solution)/shard_map/ppermute | solution.py:39
  100.1 4.6 %collective-permute-done.8 = bf16[16,3584]{1,0:T(8,128)(2,1)S(1)} collective-permute-done((bf16[16,3584]{1,0:T(8,128)(2,1)S(1)}, bf16[16,3584]{1,0:T(8,128)(2,1)S(1)}, u32[]{:S(2)}, u32[]{:S(2)}) %collective-permute-start.8) | collective-permute-done | bytes 114720 | tf_op jit(solution)/shard_map/ppermute | solution.py:35
  104.7 0.7 add_convert_fusion
  (1 shorter events, 0.0 us)
Async XLA Ops:
  1.0 4.2 %collective-permute-start = (bf16[16,3712]{1,0:T(8,128)(2,1)S(1)}, bf16[16,3712]{1,0:T(8,128)(2,1)S(1)}, u32[]{:S(2)}, u32[]{:S(2)}) collective-permute-start(bf16[16,3712]{1,0:T(8,128)(2,1)S(1)} %extend.1), channel_id=1, source_target_pairs={{0,1},{1,0},{2,3},{3,2},{4,5},{5,4},{6,7},{7,6},{8,9},{9,8},{10,11... | collective-permute-start | bytes 356360 | tf_op jit(solution)/shard_map/ppermute | solution.py:43
  4.3 17.6 %collective-permute-start.3 = (bf16[3584,512]{1,0:T(8,128)(2,1)}, bf16[3584,512]{1,0:T(8,128)(2,1)S(1)}, u32[]{:S(2)}, u32[]{:S(2)}) collective-permute-start(bf16[3584,512]{1,0:T(8,128)(2,1)} %bitcast.13), channel_id=1, source_target_pairs={{0,1},{1,0},{2,3},{3,2},{4,5},{5,4},{6,7},{7,6},{8,9},{9,8},{10,11... | collective-permute-start | bytes 11010056 | tf_op jit(solution)/shard_map/ppermute | solution.py:43
  5.3 16.6 %collective-permute-start.4 = (bf16[3584,512]{1,0:T(8,128)(2,1)}, bf16[3584,512]{1,0:T(8,128)(2,1)S(1)}, u32[]{:S(2)}, u32[]{:S(2)}) collective-permute-start(bf16[3584,512]{1,0:T(8,128)(2,1)} %bitcast.15), channel_id=1, source_target_pairs={{0,1},{1,0},{2,3},{3,2},{4,5},{5,4},{6,7},{7,6},{8,9},{9,8},{10,11... | collective-permute-start | bytes 11010056 | tf_op jit(solution)/shard_map/ppermute | solution.py:43
  5.6 16.3 %collective-permute-start.5 = (bf16[512,3584]{1,0:T(8,128)(2,1)}, bf16[512,3584]{1,0:T(8,128)(2,1)S(1)}, u32[]{:S(2)}, u32[]{:S(2)}) collective-permute-start(bf16[512,3584]{1,0:T(8,128)(2,1)} %bitcast.17), channel_id=1, source_target_pairs={{0,1},{1,0},{2,3},{3,2},{4,5},{5,4},{6,7},{7,6},{8,9},{9,8},{10,11... | collective-permute-start | bytes 11010056 | tf_op jit(solution)/shard_map/ppermute | solution.py:43
  5.8 15.2 %collective-permute-start.1 = (bf16[32,3712]{1,0:T(8,128)(2,1)S(1)}, bf16[32,3712]{1,0:T(8,128)(2,1)S(1)}, u32[]{:S(2)}, u32[]{:S(2)}) collective-permute-start(bf16[32,3712]{1,0:T(8,128)(2,1)S(1)} %pad_maximum_fusion.refs_0_), channel_id=1, source_target_pairs={{0,64},{1,193},{64,128},{65,1},{128,192},{129,65},{192,0},{193,129... | collective-permute-start | bytes 712712 | tf_op jit(solution)/shard_map/ppermute | solution.py:35
  10.2 10.8 %collective-permute-start.2 = (bf16[16,3712]{1,0:T(8,128)(2,1)S(1)}, bf16[16,3712]{1,0:T(8,128)(2,1)S(1)}, u32[]{:S(2)}, u32[]{:S(2)}) collective-permute-start(bf16[16,3712]{1,0:T(8,128)(2,1)S(1)} %extend.1), channel_id=1, source_target_pairs={{0,128},{1,129},{64,192},{65,193},{128,0},{129,1},{192,64},{193,65... | collective-permute-start | bytes 356360 | tf_op jit(solution)/shard_map/ppermute | solution.py:35
  89.9 8.4 %collective-permute-start.6 = (bf16[16,3584]{1,0:T(8,128)(2,1)S(1)}, bf16[16,3584]{1,0:T(8,128)(2,1)S(1)}, u32[]{:S(2)}, u32[]{:S(2)}) collective-permute-start(bf16[16,3584]{1,0:T(8,128)(2,1)S(1)} %get-tuple-element.30), channel_id=1, source_target_pairs={{0,192},{1,65},{64,0},{65,129},{128,64},{129,193},{192,128},{193,1... | collective-permute-start | bytes 344072 | tf_op jit(solution)/shard_map/ppermute | solution.py:35
  90.0 10.2 %collective-permute-start.7 = (bf16[16,3584]{1,0:T(8,128)(2,1)S(1)}, bf16[16,3584]{1,0:T(8,128)(2,1)S(1)}, u32[]{:S(2)}, u32[]{:S(2)}) collective-permute-start(bf16[16,3584]{1,0:T(8,128)(2,1)S(1)} %get-tuple-element.31), channel_id=1, source_target_pairs={{0,193},{1,64},{64,1},{65,128},{128,65},{129,192},{192,129},{193,0... | collective-permute-start | bytes 344072 | tf_op jit(solution)/shard_map/ppermute | solution.py:39
  94.0 10.8 %collective-permute-start.8 = (bf16[16,3584]{1,0:T(8,128)(2,1)S(1)}, bf16[16,3584]{1,0:T(8,128)(2,1)S(1)}, u32[]{:S(2)}, u32[]{:S(2)}) collective-permute-start(bf16[16,3584]{1,0:T(8,128)(2,1)S(1)} %get-tuple-element.32), channel_id=1, source_target_pairs={{0,128},{1,129},{64,192},{65,193},{128,0},{129,1},{192,64},{193,65... | collective-permute-start | bytes 344072 | tf_op jit(solution)/shard_map/ppermute | solution.py:35

commit v6 on v5

--- a/solution.py
+++ b/solution.py
@@ -234,7 +234,7 @@
     own = extend(tokens, expert_ids, gates)
     other, sent_weights = lax.optimization_barrier((swap(own), own_weights[1:]))
     other_weights = [swap(w) for w in own_weights[:1] + sent_weights]
-    own_weights = [pltpu.with_memory_space_constraint(w, pltpu.HBM) for w in own_weights]
+    own_weights[1:] = [pltpu.with_memory_space_constraint(w, pltpu.HBM) for w in own_weights[1:]]
 
     both = jnp.concatenate([own, other], axis=0)
     far = send(own, 2)
@@ -244,12 +244,12 @@
     other_weights = [pltpu.with_memory_space_constraint(w, pltpu.VMEM) for w in other_weights]
     done = experts(exchange(rows), own_weights, other_weights)
     returned = exchange(done)
-    shapes = ((block, F32), (block, BF), (block, BF), (block, BF))
+    shapes = ((block, F32), (block, F32), (block, BF), (block, BF))
     q_own, q_near, q_near_other, q_far = collect(returned, high, low, shapes)
-    far = send(q_far, -2)
-    near = send(q_near, -1)
+    far = send(q_far, -1)
     near_other = back_across(q_near_other, 1)
-    return (q_own + near.astype(F32) + near_other.astype(F32) + far.astype(F32)).astype(BF)
+    near = send((q_near + far.astype(F32)).astype(BF), -1)
+    return (q_own + near_other.astype(F32) + near.astype(F32)).astype(BF)
 
 
 def solution(mesh):

time: 107 us -> 106 us (level); the launches traced: 105 us -> 106 us
  waiting for transfers between devices: 17.2 us -> 21.7 us
  starting transfers between devices: 17.5 us -> 13.3 us
    ppermute x4, starting transfers between devices: 9.75 us -> 5.52 us  [send(): return lax.ppermute(value, ('s', 'c'), along(shift))]
    ppermute x4, waiting for transfers between devices: 14.4 us -> 17.7 us  [send(): return lax.ppermute(value, ('s', 'c'), along(shift))]
    ppermute x1, waiting for transfers between devices: 1.87 us -> 3.1 us  [back_across(): return lax.ppermute(value, ('s', 'c'), across(shift))]
  transfers between devices with their start and end apart: 9 -> 9, of which waited for: 4 -> 5; matrix products, arithmetic and copies ran while one was open for 0% -> 0% of each run, Pallas kernels for 1% -> 1%
where the time goes in v6:
time: 106 us
  blocking collectives  59.9 us (57%)
  waiting for transfers between devices  21.7 us (20%)
  starting transfers between devices  13.3 us (13%)
  Pallas kernels  9.99 us (9%)
    all_to_all x2, blocking collectives, exchange(): lax.all_to_all(blocks, names, 0, 0, axis_index_groups=groups(), tiled=True)  59.9 us
    ppermute x4, waiting for transfers between devices, send(): return lax.ppermute(value, ('s', 'c'), along(shift))  17.7 us
    pallas_call x1, Pallas kernels, experts(): pl.pallas_call(expert_kernel, out_shape=jax.ShapeDtypeStruct(rows.shape,...  7.14 us
    ppermute x4, starting transfers between devices, send(): return lax.ppermute(value, ('s', 'c'), along(shift))  5.52 us
    ppermute x1, starting transfers between devices, back_across(): return lax.ppermute(value, ('s', 'c'), across(shift))  4 us
    ppermute x4, starting transfers between devices, swap(): return lax.ppermute(value, 'c', [(0, 1), (1, 0)])  3.83 us
    ppermute x1, waiting for transfers between devices, back_across(): return lax.ppermute(value, ('s', 'c'), across(shift))  3.1 us
  transfers between devices with their start and end apart: 9, of which 5 were waited for; matrix products, arithmetic and copies ran while one was open for 0% of the time, Pallas kernels for 1%

profile of v6, /device:TPU:1, one launch (start us, length us, event | category | flops | bytes accessed | tf_op | source)
XLA Modules:
  0.0 105.7 jit_solution(2486208995741039283)
XLA Ops:
  0.0 0.0 copy-start
  0.0 1.2 %extend.1 = bf16[16,3712]{1,0:T(8,128)(2,1)S(1)} custom-call(bf16[16,3584]{1,0:T(8,128)(2,1)} %tokens.1, s32[8,16]{1,0:T(8,128)} %bitcast.19, f32[8,16]{1,0:T(8,128)} %bitcast.20), custom_call_target="tpu_custom_call" | custom-call | tf_op jit(solution)/shard_map/extend/pallas_call | solution.py:67
  1.2 3.2 %collective-permute-start = (bf16[16,3712]{1,0:T(8,128)(2,1)S(1)}, bf16[16,3712]{1,0:T(8,128)(2,1)S(1)}, u32[]{:S(2)}, u32[]{:S(2)}) collective-permute-start(bf16[16,3712]{1,0:T(8,128)(2,1)S(1)} %extend.1), channel_id=1, source_target_pairs={{0,1},{1,0},{2,3},{3,2},{4,5},{5,4},{6,7},{7,6},{8,9},{9,8},{10,11... | collective-permute-start | bytes 356360 | tf_op jit(solution)/shard_map/ppermute | solution.py:43
  4.4 0.1 collective-permute-start.3
  4.5 0.9 collective-permute-done
  5.4 0.4 collective-permute-start.4
  5.8 0.2 collective-permute-start.5
  5.9 4.4 %collective-permute-start.1 = (bf16[32,3712]{1,0:T(8,128)(2,1)S(1)}, bf16[32,3712]{1,0:T(8,128)(2,1)S(1)}, u32[]{:S(2)}, u32[]{:S(2)}) collective-permute-start(bf16[32,3712]{1,0:T(8,128)(2,1)S(1)} %pad_maximum_fusion.refs_0_), channel_id=1, source_target_pairs={{0,64},{1,193},{64,128},{65,1},{128,192},{129,65},{192,0},{193,129... | collective-permute-start | bytes 712712 | tf_op jit(solution)/shard_map/ppermute | solution.py:35
  10.3 1.0 collective-permute-start.2
  11.3 9.8 %collective-permute-done.2.refs_2_ = bf16[16,3712]{1,0:T(8,128)(2,1)S(1)} collective-permute-done((bf16[16,3712]{1,0:T(8,128)(2,1)S(1)}, bf16[16,3712]{1,0:T(8,128)(2,1)S(1)}, u32[]{:S(2)}, u32[]{:S(2)}) %collective-permute-start.2) | collective-permute-done | bytes 118816 | tf_op jit(solution)/shard_map/ppermute | solution.py:35
  21.1 0.0 collective-permute-done.1.refs_1_
  21.1 0.9 place.1
  22.0 0.0 collective-permute-done.3.gate_b
  22.0 0.0 collective-permute-done.4.up_b
  22.0 0.0 collective-permute-done.5.down_b
  22.1 30.6 %all_to_all.10 = bf16[32,8,3584]{2,1,0:T(8,128)(2,1)S(1)} all-to-all(bf16[32,8,3584]{2,1,0:T(8,128)(2,1)S(1)} %bitcast.14), channel_id=1, replica_groups={{0,8,16,24,32,40,48,56,2,10,18,26,34,42,50,58,4,12,20,28,36,44,52,60,6,..., dimensions={0} | all-to-all | bytes 3670016 | tf_op jit(solution)/shard_map/all_to_all | solution.py:228
  52.6 0.0 copy-done
  52.6 7.1 %experts.1 = bf16[256,3584]{1,0:T(8,128)(2,1)S(1)} custom-call(bf16[256,3584]{1,0:T(8,128)(2,1)S(1)} %bitcast.9, bf16[3584,512]{1,0:T(8,128)(2,1)S(1)} %bitcast.13, bf16[3584,512]{1,0:T(8,128)(2,1)} %bitcast.16, bf16[512,3584]{1,0:T(8,128)(2,1)} %bitcast.18, bf16[3584,512]{1,0:T(8,128)(2,1)S(1)} %collective-permute-done.3.gate_b, ...), custom_call_target="tpu_custom_call" | custom-call | flops 5637144576 | bytes 25690112 | tf_op jit(solution)/shard_map/experts/pallas_call | solution.py:167
  59.8 29.3 %all_to_all.11 = bf16[32,8,3584]{2,1,0:T(8,128)(2,1)S(1)} all-to-all(bf16[32,8,3584]{2,1,0:T(8,128)(2,1)S(1)} %bitcast.10), channel_id=1, replica_groups={{0,8,16,24,32,40,48,56,2,10,18,26,34,42,50,58,4,12,20,28,36,44,52,60,6,..., dimensions={0} | all-to-all | bytes 3670016 | tf_op jit(solution)/shard_map/all_to_all | solution.py:228
  89.1 0.8 collect.1
  89.8 0.1 collective-permute-start.7
  89.9 4.0 %collective-permute-start.6 = (bf16[16,3584]{1,0:T(8,128)(2,1)S(1)}, bf16[16,3584]{1,0:T(8,128)(2,1)S(1)}, u32[]{:S(2)}, u32[]{:S(2)}) collective-permute-start(bf16[16,3584]{1,0:T(8,128)(2,1)S(1)} %get-tuple-element.30), channel_id=1, source_target_pairs={{0,193},{1,64},{64,1},{65,128},{128,65},{129,192},{192,129},{193,0... | collective-permute-start | bytes 344072 | tf_op jit(solution)/shard_map/ppermute | solution.py:39
  93.9 3.0 %collective-permute-done.7 = bf16[16,3584]{1,0:T(8,128)(2,1)S(1)} collective-permute-done((bf16[16,3584]{1,0:T(8,128)(2,1)S(1)}, bf16[16,3584]{1,0:T(8,128)(2,1)S(1)}, u32[]{:S(2)}, u32[]{:S(2)}) %collective-permute-start.7) | collective-permute-done | bytes 114720 | tf_op jit(solution)/shard_map/ppermute | solution.py:35
  96.9 0.1 collective-permute-start.8
  97.0 3.1 %collective-permute-done.6 = bf16[16,3584]{1,0:T(8,128)(2,1)S(1)} collective-permute-done((bf16[16,3584]{1,0:T(8,128)(2,1)S(1)}, bf16[16,3584]{1,0:T(8,128)(2,1)S(1)}, u32[]{:S(2)}, u32[]{:S(2)}) %collective-permute-start.6) | collective-permute-done | bytes 114720 | tf_op jit(solution)/shard_map/ppermute | solution.py:39
  100.1 4.9 %collective-permute-done.8 = bf16[16,3584]{1,0:T(8,128)(2,1)S(1)} collective-permute-done((bf16[16,3584]{1,0:T(8,128)(2,1)S(1)}, bf16[16,3584]{1,0:T(8,128)(2,1)S(1)}, u32[]{:S(2)}, u32[]{:S(2)}) %collective-permute-start.8) | collective-permute-done | bytes 114720 | tf_op jit(solution)/shard_map/ppermute | solution.py:35
  105.0 0.7 add_convert_fusion
  (2 shorter events, 0.0 us)
Async XLA Ops:
  0.0 52.6 %copy-start = (bf16[1,3584,512]{2,1,0:T(8,128)(2,1)S(1)}, bf16[1,3584,512]{2,1,0:T(8,128)(2,1)}, u32[]{:S(2)}) copy-start(bf16[1,3584,512]{2,1,0:T(8,128)(2,1)} %param.9) | copy-start | bytes 11010052
  1.2 4.2 %collective-permute-start = (bf16[16,3712]{1,0:T(8,128)(2,1)S(1)}, bf16[16,3712]{1,0:T(8,128)(2,1)S(1)}, u32[]{:S(2)}, u32[]{:S(2)}) collective-permute-start(bf16[16,3712]{1,0:T(8,128)(2,1)S(1)} %extend.1), channel_id=1, source_target_pairs={{0,1},{1,0},{2,3},{3,2},{4,5},{5,4},{6,7},{7,6},{8,9},{9,8},{10,11... | collective-permute-start | bytes 356360 | tf_op jit(solution)/shard_map/ppermute | solution.py:43
  4.4 17.6 %collective-permute-start.3 = (bf16[3584,512]{1,0:T(8,128)(2,1)}, bf16[3584,512]{1,0:T(8,128)(2,1)S(1)}, u32[]{:S(2)}, u32[]{:S(2)}) collective-permute-start(bf16[3584,512]{1,0:T(8,128)(2,1)} %bitcast.12), channel_id=1, source_target_pairs={{0,1},{1,0},{2,3},{3,2},{4,5},{5,4},{6,7},{7,6},{8,9},{9,8},{10,11... | collective-permute-start | bytes 11010056 | tf_op jit(solution)/shard_map/ppermute | solution.py:43
  5.4 16.6 %collective-permute-start.4 = (bf16[3584,512]{1,0:T(8,128)(2,1)}, bf16[3584,512]{1,0:T(8,128)(2,1)S(1)}, u32[]{:S(2)}, u32[]{:S(2)}) collective-permute-start(bf16[3584,512]{1,0:T(8,128)(2,1)} %bitcast.15), channel_id=1, source_target_pairs={{0,1},{1,0},{2,3},{3,2},{4,5},{5,4},{6,7},{7,6},{8,9},{9,8},{10,11... | collective-permute-start | bytes 11010056 | tf_op jit(solution)/shard_map/ppermute | solution.py:43
  5.8 16.3 %collective-permute-start.5 = (bf16[512,3584]{1,0:T(8,128)(2,1)}, bf16[512,3584]{1,0:T(8,128)(2,1)S(1)}, u32[]{:S(2)}, u32[]{:S(2)}) collective-permute-start(bf16[512,3584]{1,0:T(8,128)(2,1)} %bitcast.17), channel_id=1, source_target_pairs={{0,1},{1,0},{2,3},{3,2},{4,5},{5,4},{6,7},{7,6},{8,9},{9,8},{10,11... | collective-permute-start | bytes 11010056 | tf_op jit(solution)/shard_map/ppermute | solution.py:43
  5.9 15.2 %collective-permute-start.1 = (bf16[32,3712]{1,0:T(8,128)(2,1)S(1)}, bf16[32,3712]{1,0:T(8,128)(2,1)S(1)}, u32[]{:S(2)}, u32[]{:S(2)}) collective-permute-start(bf16[32,3712]{1,0:T(8,128)(2,1)S(1)} %pad_maximum_fusion.refs_0_), channel_id=1, source_target_pairs={{0,64},{1,193},{64,128},{65,1},{128,192},{129,65},{192,0},{193,129... | collective-permute-start | bytes 712712 | tf_op jit(solution)/shard_map/ppermute | solution.py:35
  10.3 10.8 %collective-permute-start.2 = (bf16[16,3712]{1,0:T(8,128)(2,1)S(1)}, bf16[16,3712]{1,0:T(8,128)(2,1)S(1)}, u32[]{:S(2)}, u32[]{:S(2)}) collective-permute-start(bf16[16,3712]{1,0:T(8,128)(2,1)S(1)} %extend.1), channel_id=1, source_target_pairs={{0,128},{1,129},{64,192},{65,193},{128,0},{129,1},{192,64},{193,65... | collective-permute-start | bytes 356360 | tf_op jit(solution)/shard_map/ppermute | solution.py:35
  89.8 7.1 %collective-permute-start.7 = (bf16[16,3584]{1,0:T(8,128)(2,1)S(1)}, bf16[16,3584]{1,0:T(8,128)(2,1)S(1)}, u32[]{:S(2)}, u32[]{:S(2)}) collective-permute-start(bf16[16,3584]{1,0:T(8,128)(2,1)S(1)} %get-tuple-element.32), channel_id=1, source_target_pairs={{0,192},{1,65},{64,0},{65,129},{128,64},{129,193},{192,128},{193,1... | collective-permute-start | bytes 344072 | tf_op jit(solution)/shard_map/ppermute | solution.py:35
  89.9 10.2 %collective-permute-start.6 = (bf16[16,3584]{1,0:T(8,128)(2,1)S(1)}, bf16[16,3584]{1,0:T(8,128)(2,1)S(1)}, u32[]{:S(2)}, u32[]{:S(2)}) collective-permute-start(bf16[16,3584]{1,0:T(8,128)(2,1)S(1)} %get-tuple-element.30), channel_id=1, source_target_pairs={{0,193},{1,64},{64,1},{65,128},{128,65},{129,192},{192,129},{193,0... | collective-permute-start | bytes 344072 | tf_op jit(solution)/shard_map/ppermute | solution.py:39
  96.9 8.1 %collective-permute-start.8 = (bf16[16,3584]{1,0:T(8,128)(2,1)S(1)}, bf16[16,3584]{1,0:T(8,128)(2,1)S(1)}, u32[]{:S(2)}, u32[]{:S(2)}) collective-permute-start(bf16[16,3584]{1,0:T(8,128)(2,1)S(1)} %add_convert_fusion.1), channel_id=1, source_target_pairs={{0,192},{1,65},{64,0},{65,129},{128,64},{129,193},{192,128},{193,1... | collective-permute-start | bytes 344072 | tf_op jit(solution)/shard_map/ppermute | solution.py:35

commit v7 on v6

--- a/solution.py
+++ b/solution.py
@@ -232,8 +232,8 @@
     block, width = tokens.shape
     own_weights = [gate_weight[0], up_weight[0], down_weight[0]]
     own = extend(tokens, expert_ids, gates)
-    other, sent_weights = lax.optimization_barrier((swap(own), own_weights[1:]))
-    other_weights = [swap(w) for w in own_weights[:1] + sent_weights]
+    other, sent_weights = lax.optimization_barrier((swap(own), own_weights[2:]))
+    other_weights = [swap(w) for w in own_weights[:2] + sent_weights]
     own_weights[1:] = [pltpu.with_memory_space_constraint(w, pltpu.HBM) for w in own_weights[1:]]
 
     both = jnp.concatenate([own, other], axis=0)

time: 106 us -> 106 us (level)
  blocking collectives: 59.9 us -> 58.7 us
    all_to_all x2, blocking collectives: 59.9 us -> 58.7 us  [exchange(): lax.all_to_all(blocks, names, 0, 0, axis_index_groups=groups(), tiled=True)]
where the time goes in v7:
time: 106 us; the launch traced here: 105 us
  blocking collectives  58.7 us (55%)
  waiting for transfers between devices  21.4 us (20%)
  starting transfers between devices  14.2 us (13%)
  Pallas kernels  9.99 us (9%)
    all_to_all x2, blocking collectives, exchange(): lax.all_to_all(blocks, names, 0, 0, axis_index_groups=groups(), tiled=True)  58.7 us
    ppermute x4, waiting for transfers between devices, send(): return lax.ppermute(value, ('s', 'c'), along(shift))  17 us
    pallas_call x1, Pallas kernels, experts(): pl.pallas_call(expert_kernel, out_shape=jax.ShapeDtypeStruct(rows.shape,...  7.14 us
    ppermute x4, starting transfers between devices, send(): return lax.ppermute(value, ('s', 'c'), along(shift))  6.55 us
    ppermute x4, starting transfers between devices, swap(): return lax.ppermute(value, 'c', [(0, 1), (1, 0)])  4.11 us
    ppermute x1, waiting for transfers between devices, back_across(): return lax.ppermute(value, ('s', 'c'), across(shift))  3.95 us
    ppermute x1, starting transfers between devices, back_across(): return lax.ppermute(value, ('s', 'c'), across(shift))  3.52 us
  transfers between devices with their start and end apart: 9, of which 5 were waited for; matrix products, arithmetic and copies ran while one was open for 0% of the time, Pallas kernels for 1%

profile of v7, /device:TPU:1, one launch (start us, length us, event | category | flops | bytes accessed | tf_op | source)
XLA Modules:
  0.0 105.1 jit_solution(14395623082197710240)
XLA Ops:
  0.0 0.0 copy-start
  0.0 1.2 %extend.1 = bf16[16,3712]{1,0:T(8,128)(2,1)S(1)} custom-call(bf16[16,3584]{1,0:T(8,128)(2,1)} %tokens.1, s32[8,16]{1,0:T(8,128)} %bitcast.19, f32[8,16]{1,0:T(8,128)} %bitcast.20), custom_call_target="tpu_custom_call" | custom-call | tf_op jit(solution)/shard_map/extend/pallas_call | solution.py:67
  1.2 3.2 %collective-permute-start = (bf16[16,3712]{1,0:T(8,128)(2,1)S(1)}, bf16[16,3712]{1,0:T(8,128)(2,1)S(1)}, u32[]{:S(2)}, u32[]{:S(2)}) collective-permute-start(bf16[16,3712]{1,0:T(8,128)(2,1)S(1)} %extend.1), channel_id=1, source_target_pairs={{0,1},{1,0},{2,3},{3,2},{4,5},{5,4},{6,7},{7,6},{8,9},{9,8},{10,11... | collective-permute-start | bytes 356360 | tf_op jit(solution)/shard_map/ppermute | solution.py:43
  4.4 0.1 collective-permute-start.3
  4.5 0.4 collective-permute-start.4
  5.0 0.5 collective-permute-done
  5.4 0.4 collective-permute-start.5
  5.8 4.4 %collective-permute-start.1 = (bf16[32,3712]{1,0:T(8,128)(2,1)S(1)}, bf16[32,3712]{1,0:T(8,128)(2,1)S(1)}, u32[]{:S(2)}, u32[]{:S(2)}) collective-permute-start(bf16[32,3712]{1,0:T(8,128)(2,1)S(1)} %pad_maximum_fusion.refs_0_), channel_id=1, source_target_pairs={{0,64},{1,193},{64,128},{65,1},{128,192},{129,65},{192,0},{193,129... | collective-permute-start | bytes 712712 | tf_op jit(solution)/shard_map/ppermute | solution.py:35
  10.2 1.0 collective-permute-start.2
  11.1 10.6 %collective-permute-done.2.refs_2_ = bf16[16,3712]{1,0:T(8,128)(2,1)S(1)} collective-permute-done((bf16[16,3712]{1,0:T(8,128)(2,1)S(1)}, bf16[16,3712]{1,0:T(8,128)(2,1)S(1)}, u32[]{:S(2)}, u32[]{:S(2)}) %collective-permute-start.2) | collective-permute-done | bytes 118816 | tf_op jit(solution)/shard_map/ppermute | solution.py:35
  21.7 0.0 collective-permute-done.1.refs_1_
  21.7 0.9 place.1
  22.6 0.0 collective-permute-done.3.gate_b
  22.6 0.0 collective-permute-done.4.up_b
  22.6 0.0 collective-permute-done.5.down_b
  22.6 29.9 %all_to_all.10 = bf16[32,8,3584]{2,1,0:T(8,128)(2,1)S(1)} all-to-all(bf16[32,8,3584]{2,1,0:T(8,128)(2,1)S(1)} %bitcast.14), channel_id=1, replica_groups={{0,8,16,24,32,40,48,56,2,10,18,26,34,42,50,58,4,12,20,28,36,44,52,60,6,..., dimensions={0} | all-to-all | bytes 3670016 | tf_op jit(solution)/shard_map/all_to_all | solution.py:228
  52.5 0.0 copy-done
  52.5 7.1 %experts.1 = bf16[256,3584]{1,0:T(8,128)(2,1)S(1)} custom-call(bf16[256,3584]{1,0:T(8,128)(2,1)S(1)} %bitcast.9, bf16[3584,512]{1,0:T(8,128)(2,1)S(1)} %bitcast.13, bf16[3584,512]{1,0:T(8,128)(2,1)} %bitcast.16, bf16[512,3584]{1,0:T(8,128)(2,1)} %bitcast.18, bf16[3584,512]{1,0:T(8,128)(2,1)S(1)} %collective-permute-done.3.gate_b, ...), custom_call_target="tpu_custom_call" | custom-call | flops 5637144576 | bytes 25690112 | tf_op jit(solution)/shard_map/experts/pallas_call | solution.py:167
  59.7 28.8 %all_to_all.11 = bf16[32,8,3584]{2,1,0:T(8,128)(2,1)S(1)} all-to-all(bf16[32,8,3584]{2,1,0:T(8,128)(2,1)S(1)} %bitcast.10), channel_id=1, replica_groups={{0,8,16,24,32,40,48,56,2,10,18,26,34,42,50,58,4,12,20,28,36,44,52,60,6,..., dimensions={0} | all-to-all | bytes 3670016 | tf_op jit(solution)/shard_map/all_to_all | solution.py:228
  88.5 0.8 collect.1
  89.3 1.1 %collective-permute-start.7 = (bf16[16,3584]{1,0:T(8,128)(2,1)S(1)}, bf16[16,3584]{1,0:T(8,128)(2,1)S(1)}, u32[]{:S(2)}, u32[]{:S(2)}) collective-permute-start(bf16[16,3584]{1,0:T(8,128)(2,1)S(1)} %get-tuple-element.30), channel_id=1, source_target_pairs={{0,192},{1,65},{64,0},{65,129},{128,64},{129,193},{192,128},{193,1... | collective-permute-start | bytes 344072 | tf_op jit(solution)/shard_map/ppermute | solution.py:35
  90.4 3.5 %collective-permute-start.6 = (bf16[16,3584]{1,0:T(8,128)(2,1)S(1)}, bf16[16,3584]{1,0:T(8,128)(2,1)S(1)}, u32[]{:S(2)}, u32[]{:S(2)}) collective-permute-start(bf16[16,3584]{1,0:T(8,128)(2,1)S(1)} %get-tuple-element.28), channel_id=1, source_target_pairs={{0,193},{1,64},{64,1},{65,128},{128,65},{129,192},{192,129},{193,0... | collective-permute-start | bytes 344072 | tf_op jit(solution)/shard_map/ppermute | solution.py:39
  93.9 2.4 %collective-permute-done.7 = bf16[16,3584]{1,0:T(8,128)(2,1)S(1)} collective-permute-done((bf16[16,3584]{1,0:T(8,128)(2,1)S(1)}, bf16[16,3584]{1,0:T(8,128)(2,1)S(1)}, u32[]{:S(2)}, u32[]{:S(2)}) %collective-permute-start.7) | collective-permute-done | bytes 114720 | tf_op jit(solution)/shard_map/ppermute | solution.py:35
  96.3 0.1 collective-permute-start.8
  96.4 4.0 %collective-permute-done.6 = bf16[16,3584]{1,0:T(8,128)(2,1)S(1)} collective-permute-done((bf16[16,3584]{1,0:T(8,128)(2,1)S(1)}, bf16[16,3584]{1,0:T(8,128)(2,1)S(1)}, u32[]{:S(2)}, u32[]{:S(2)}) %collective-permute-start.6) | collective-permute-done | bytes 114720 | tf_op jit(solution)/shard_map/ppermute | solution.py:39
  100.4 4.1 %collective-permute-done.8 = bf16[16,3584]{1,0:T(8,128)(2,1)S(1)} collective-permute-done((bf16[16,3584]{1,0:T(8,128)(2,1)S(1)}, bf16[16,3584]{1,0:T(8,128)(2,1)S(1)}, u32[]{:S(2)}, u32[]{:S(2)}) %collective-permute-start.8) | collective-permute-done | bytes 114720 | tf_op jit(solution)/shard_map/ppermute | solution.py:35
  104.4 0.7 add_convert_fusion
  (2 shorter events, 0.0 us)
Async XLA Ops:
  0.0 52.5 %copy-start = (bf16[1,3584,512]{2,1,0:T(8,128)(2,1)S(1)}, bf16[1,3584,512]{2,1,0:T(8,128)(2,1)}, u32[]{:S(2)}) copy-start(bf16[1,3584,512]{2,1,0:T(8,128)(2,1)} %param.9) | copy-start | bytes 11010052
  1.2 4.2 %collective-permute-start = (bf16[16,3712]{1,0:T(8,128)(2,1)S(1)}, bf16[16,3712]{1,0:T(8,128)(2,1)S(1)}, u32[]{:S(2)}, u32[]{:S(2)}) collective-permute-start(bf16[16,3712]{1,0:T(8,128)(2,1)S(1)} %extend.1), channel_id=1, source_target_pairs={{0,1},{1,0},{2,3},{3,2},{4,5},{5,4},{6,7},{7,6},{8,9},{9,8},{10,11... | collective-permute-start | bytes 356360 | tf_op jit(solution)/shard_map/ppermute | solution.py:43
  4.4 18.1 %collective-permute-start.3 = (bf16[3584,512]{1,0:T(8,128)(2,1)}, bf16[3584,512]{1,0:T(8,128)(2,1)S(1)}, u32[]{:S(2)}, u32[]{:S(2)}) collective-permute-start(bf16[3584,512]{1,0:T(8,128)(2,1)} %bitcast.12), channel_id=1, source_target_pairs={{0,1},{1,0},{2,3},{3,2},{4,5},{5,4},{6,7},{7,6},{8,9},{9,8},{10,11... | collective-permute-start | bytes 11010056 | tf_op jit(solution)/shard_map/ppermute | solution.py:43
  4.5 18.1 %collective-permute-start.4 = (bf16[3584,512]{1,0:T(8,128)(2,1)}, bf16[3584,512]{1,0:T(8,128)(2,1)S(1)}, u32[]{:S(2)}, u32[]{:S(2)}) collective-permute-start(bf16[3584,512]{1,0:T(8,128)(2,1)} %bitcast.15), channel_id=1, source_target_pairs={{0,1},{1,0},{2,3},{3,2},{4,5},{5,4},{6,7},{7,6},{8,9},{9,8},{10,11... | collective-permute-start | bytes 11010056 | tf_op jit(solution)/shard_map/ppermute | solution.py:43
  5.4 17.2 %collective-permute-start.5 = (bf16[512,3584]{1,0:T(8,128)(2,1)}, bf16[512,3584]{1,0:T(8,128)(2,1)S(1)}, u32[]{:S(2)}, u32[]{:S(2)}) collective-permute-start(bf16[512,3584]{1,0:T(8,128)(2,1)} %bitcast.17), channel_id=1, source_target_pairs={{0,1},{1,0},{2,3},{3,2},{4,5},{5,4},{6,7},{7,6},{8,9},{9,8},{10,11... | collective-permute-start | bytes 11010056 | tf_op jit(solution)/shard_map/ppermute | solution.py:43
  5.8 15.9 %collective-permute-start.1 = (bf16[32,3712]{1,0:T(8,128)(2,1)S(1)}, bf16[32,3712]{1,0:T(8,128)(2,1)S(1)}, u32[]{:S(2)}, u32[]{:S(2)}) collective-permute-start(bf16[32,3712]{1,0:T(8,128)(2,1)S(1)} %pad_maximum_fusion.refs_0_), channel_id=1, source_target_pairs={{0,64},{1,193},{64,128},{65,1},{128,192},{129,65},{192,0},{193,129... | collective-permute-start | bytes 712712 | tf_op jit(solution)/shard_map/ppermute | solution.py:35
  10.2 11.5 %collective-permute-start.2 = (bf16[16,3712]{1,0:T(8,128)(2,1)S(1)}, bf16[16,3712]{1,0:T(8,128)(2,1)S(1)}, u32[]{:S(2)}, u32[]{:S(2)}) collective-permute-start(bf16[16,3712]{1,0:T(8,128)(2,1)S(1)} %extend.1), channel_id=1, source_target_pairs={{0,128},{1,129},{64,192},{65,193},{128,0},{129,1},{192,64},{193,65... | collective-permute-start | bytes 356360 | tf_op jit(solution)/shard_map/ppermute | solution.py:35
  89.3 7.0 %collective-permute-start.7 = (bf16[16,3584]{1,0:T(8,128)(2,1)S(1)}, bf16[16,3584]{1,0:T(8,128)(2,1)S(1)}, u32[]{:S(2)}, u32[]{:S(2)}) collective-permute-start(bf16[16,3584]{1,0:T(8,128)(2,1)S(1)} %get-tuple-element.30), channel_id=1, source_target_pairs={{0,192},{1,65},{64,0},{65,129},{128,64},{129,193},{192,128},{193,1... | collective-permute-start | bytes 344072 | tf_op jit(solution)/shard_map/ppermute | solution.py:35
  90.4 10.0 %collective-permute-start.6 = (bf16[16,3584]{1,0:T(8,128)(2,1)S(1)}, bf16[16,3584]{1,0:T(8,128)(2,1)S(1)}, u32[]{:S(2)}, u32[]{:S(2)}) collective-permute-start(bf16[16,3584]{1,0:T(8,128)(2,1)S(1)} %get-tuple-element.28), channel_id=1, source_target_pairs={{0,193},{1,64},{64,1},{65,128},{128,65},{129,192},{192,129},{193,0... | collective-permute-start | bytes 344072 | tf_op jit(solution)/shard_map/ppermute | solution.py:39
  96.3 8.1 %collective-permute-start.8 = (bf16[16,3584]{1,0:T(8,128)(2,1)S(1)}, bf16[16,3584]{1,0:T(8,128)(2,1)S(1)}, u32[]{:S(2)}, u32[]{:S(2)}) collective-permute-start(bf16[16,3584]{1,0:T(8,128)(2,1)S(1)} %add_convert_fusion.1), channel_id=1, source_target_pairs={{0,192},{1,65},{64,0},{65,129},{128,64},{129,193},{192,128},{193,1... | collective-permute-start | bytes 344072 | tf_op jit(solution)/shard_map/ppermute | solution.py:35
